TPU v7x, 256 devices: a whole 4x4x8 slice. The times are simulated.
256 devices in a mesh: space: 64 (over z, y, core), halo: 4 (over x).
Axes of the slice: x: 4, y: 4, z: 8, core: 2. Of those that a mesh axis runs over, the one named last changes fastest.
Arguments:
- positions: float32 [3, 1048576], P(None, 'space'), may hold values from -1 to 1
- masses: float32 [1048576], P('space'), may hold values from 0.1 to 10
- centres: float32 [4, 3, 1024], P('halo'), may hold values from -0.5 to 0.5
- pair_halo: int32 [4, 16384], P('halo', 'space'), may hold values from 0 to 1023
- pair_tile: int32 [4, 16384], P('halo', 'space'), may hold values from 0 to 31
- halo_slot: int32 [4, 1024], P('halo'), may hold values from 0 to 1023, each once within a row
- feedback: float32 [4, 1024], P('halo', 'space'), may hold values from 0.5 to 1.5
- mixing: float32 [3, 128, 128], replicated, may hold values from -0.5 to 0.5
- drive: float32 [3, 128], replicated, may hold values from 0.2 to 1
- readout: float32 [3, 128], replicated, may hold values from -1.5 to 1.5
Outputs:
- displacement: float32 [3, 1048576], P(None, 'space')
All inputs are finite; a program needn't handle non-finite values.
Results may differ from a plain program's by a relative error of at most 0.0003.
Values sent between devices are 32-bit elements; how exact they have to be, the bound alone decides.
A program may use at most 64 MiB of HBM per device.

v0:
```python
import jax
import jax.numpy as jnp
from jax import lax
from jax.sharding import PartitionSpec as P

BLK = 512
ITERS = 8


def split_up(x, dim, length):
    before, after = (x.shape[:dim], x.shape[dim + 1 :])
    return jnp.moveaxis(x.reshape(*before, length, -1, *after), dim, 0)


def sum_at_owner(x, axis, dim):
    length = lax.axis_size(axis)
    tiles = lax.all_to_all(split_up(x, dim, length), axis, 0, 0, tiled=True)
    return jnp.sum(tiles, axis=0)


def from_everyone(x, axis):
    copies = jnp.broadcast_to(x, (lax.axis_size(axis), *x.shape))
    return lax.all_to_all(copies, axis, split_axis=0, concat_axis=0, tiled=True)


def laid_out(tiles, dim):
    tiles = jnp.moveaxis(tiles, 0, dim)
    dims = tiles.shape
    return tiles.reshape(*dims[:dim], dims[dim] * dims[dim + 1], *dims[dim + 2 :])


def gather_directly(x, axis, dim):
    tiles = from_everyone(x, axis)
    return laid_out(tiles, dim)


def of_everyone(x, axis):
    everything = from_everyone(x, axis)
    return jnp.sum(everything, axis=0)


def spline_basis(offset, knots):
    radial_distance = jnp.sqrt(jnp.sum(offset * offset, axis=0))
    scaled = radial_distance * ((knots - 1) / 2.6)
    knot_index = jnp.arange(knots, dtype=jnp.float32)
    return jnp.maximum(0.0, 1.0 - jnp.abs(scaled[..., None] - knot_index))


def relax(level, phi, mixing, drive, readout):
    state = jnp.zeros((3,) + level.shape, jnp.float32)
    for relax_iteration in range(ITERS):
        average = jnp.mean(state, axis=0)
        fresh = []
        for comp in range(3):
            mixed = jnp.dot(state[comp], mixing[comp], precision=lax.Precision.HIGHEST)
            fresh.append(jnp.tanh(drive[comp] * level + phi[:, None] * mixed + 0.5 * average))
        state = jnp.stack(fresh)
    return jnp.sum(state * readout[:, None, :], axis=0)


def per_device(
    positions, masses, centres, pair_halo, pair_tile, halo_slot, feedback, mixing, drive, readout
):
    knots = mixing.shape[1]
    tile_count = masses.shape[0] // BLK
    number_of_pairs = pair_halo.shape[1]
    places = positions.reshape(3, tile_count, BLK)
    weights = masses.reshape(tile_count, BLK)
    halo_ids = pair_halo[0]
    tile_ids = pair_tile[0]
    centre_rows = centres[0]
    slot_ids = halo_slot[0][halo_ids]
    block = min(64, number_of_pairs // 8)
    offsets = places[:, tile_ids, :] - centre_rows[:, halo_ids][:, :, None]
    offset_blocks = jnp.transpose(offsets.reshape(3, -1, block, BLK), (1, 0, 2, 3))
    weight_blocks = weights[tile_ids].reshape(-1, block, BLK)

    def project(inputs):
        offset_part, weight_part = inputs
        basis = spline_basis(offset_part, knots)
        return jnp.sum(weight_part[:, :, None] * basis, axis=1)

    pair_rows = lax.map(project, (offset_blocks, weight_blocks)).reshape(number_of_pairs, knots)
    wanted = jnp.arange(feedback.shape[1] * lax.axis_size("space"), dtype=jnp.int32)
    halo_selection = (slot_ids[None, :] == wanted[:, None]).astype(jnp.float32)
    owned = sum_at_owner(
        jnp.dot(halo_selection, pair_rows, precision=lax.Precision.HIGHEST), "space", 0
    )
    owned_coef = relax(jnp.log1p(owned), feedback[0], mixing, drive, readout)
    coef_table = gather_directly(owned_coef, "space", 0)
    coef_rows = coef_table[slot_ids].reshape(-1, block, knots)

    def evaluate(inputs):
        offset_part, coef_part = inputs
        basis = spline_basis(offset_part, knots)
        scalar = jnp.sum(basis * coef_part[:, None, :], axis=2)
        return offset_part * scalar[None]

    shifted_positions = lax.map(evaluate, (offset_blocks, coef_rows))
    shifted_positions = jnp.transpose(shifted_positions, (1, 0, 2, 3)).reshape(
        3, number_of_pairs, BLK
    )
    current_tile = jnp.arange(tile_count, dtype=jnp.int32)
    halo_selection = (current_tile[:, None] == tile_ids[None, :]).astype(jnp.float32)
    partial_halo_sum = jnp.einsum(
        "dq,vqn->vdn", halo_selection, shifted_positions, precision=lax.Precision.HIGHEST
    )
    partial_halo_sum = partial_halo_sum.reshape(3, tile_count * BLK)
    return of_everyone(partial_halo_sum, "halo")


def solution(mesh):
    return jax.shard_map(
        per_device,
        mesh=mesh,
        in_specs=(
            P(None, "space"),
            P("space"),
            P("halo", None, None),
            P("halo", "space"),
            P("halo", "space"),
            P("halo", None),
            P("halo", "space"),
            P(),
            P(),
            P(),
        ),
        out_specs=P(None, "space"),
        check_vma=False,
    )
```

profile of v0, /device:TPU:1, one launch (start us, length us, event | category | flops | bytes accessed | tf_op | source)
XLA Modules:
  0.0 178.5 jit_solution(15134571292651254631)
XLA Ops:
  9.0 40.7 %while.20 = (s32[]{:T(128)}, f32[8,32,128]{2,1,0:T(8,128)S(1)}, f32[8,32,512]{2,1,0:T(8,128)S(1)}, f32[8,3,32,512]{3,2,1,0:T(8,128)S(1)}, s32[]{:T(128)}) while((s32[]{:T(128)}, f32[8,32,128]{2,1,0:T(8,128)S(1)}, f32[8,32,512]{2,1,0:T(8,128)S(1)}, f32[8,3,32,512]{3,2,1,0:T(8,128)S(1)}, s32[]{:T(128)}) %tuple.46), condition=%wide.region_3.4_spmd, body=%wide.region_0.3_spmd.sunk | while | flops 12677122 | bytes 704585 | solution.py:83
  9.1 5.0 %multiply_reduce_fusion.9 = f32[32,128]{1,0:T(8,128)S(1)} fusion(f32[32,512]{1,0:T(8,128)S(1)} %sqrt_multiply_fusion.4, f32[32,512]{1,0:T(8,128)S(1)} %dynamic-slice_bitcast_fusion.4), kind=kLoop, calls=%fused_computation.5.clone.1 | loop fusion | flops 12578816 | bytes 147456 | tf_op jit(solution)/shard_map/while/body/eval_jaxpr/reduce_sum | solution.py:81
  14.2 5.0 %multiply_reduce_fusion.9 = f32[32,128]{1,0:T(8,128)S(1)} fusion(f32[32,512]{1,0:T(8,128)S(1)} %sqrt_multiply_fusion.4, f32[32,512]{1,0:T(8,128)S(1)} %dynamic-slice_bitcast_fusion.4), kind=kLoop, calls=%fused_computation.5.clone.1 | loop fusion | flops 12578816 | bytes 147456 | tf_op jit(solution)/shard_map/while/body/eval_jaxpr/reduce_sum | solution.py:81
  19.3 5.0 %multiply_reduce_fusion.9 = f32[32,128]{1,0:T(8,128)S(1)} fusion(f32[32,512]{1,0:T(8,128)S(1)} %sqrt_multiply_fusion.4, f32[32,512]{1,0:T(8,128)S(1)} %dynamic-slice_bitcast_fusion.4), kind=kLoop, calls=%fused_computation.5.clone.1 | loop fusion | flops 12578816 | bytes 147456 | tf_op jit(solution)/shard_map/while/body/eval_jaxpr/reduce_sum | solution.py:81
  24.4 5.0 %multiply_reduce_fusion.9 = f32[32,128]{1,0:T(8,128)S(1)} fusion(f32[32,512]{1,0:T(8,128)S(1)} %sqrt_multiply_fusion.4, f32[32,512]{1,0:T(8,128)S(1)} %dynamic-slice_bitcast_fusion.4), kind=kLoop, calls=%fused_computation.5.clone.1 | loop fusion | flops 12578816 | bytes 147456 | tf_op jit(solution)/shard_map/while/body/eval_jaxpr/reduce_sum | solution.py:81
  29.5 5.0 %multiply_reduce_fusion.9 = f32[32,128]{1,0:T(8,128)S(1)} fusion(f32[32,512]{1,0:T(8,128)S(1)} %sqrt_multiply_fusion.4, f32[32,512]{1,0:T(8,128)S(1)} %dynamic-slice_bitcast_fusion.4), kind=kLoop, calls=%fused_computation.5.clone.1 | loop fusion | flops 12578816 | bytes 147456 | tf_op jit(solution)/shard_map/while/body/eval_jaxpr/reduce_sum | solution.py:81
  34.6 5.0 %multiply_reduce_fusion.9 = f32[32,128]{1,0:T(8,128)S(1)} fusion(f32[32,512]{1,0:T(8,128)S(1)} %sqrt_multiply_fusion.4, f32[32,512]{1,0:T(8,128)S(1)} %dynamic-slice_bitcast_fusion.4), kind=kLoop, calls=%fused_computation.5.clone.1 | loop fusion | flops 12578816 | bytes 147456 | tf_op jit(solution)/shard_map/while/body/eval_jaxpr/reduce_sum | solution.py:81
  39.7 5.0 %multiply_reduce_fusion.9 = f32[32,128]{1,0:T(8,128)S(1)} fusion(f32[32,512]{1,0:T(8,128)S(1)} %sqrt_multiply_fusion.4, f32[32,512]{1,0:T(8,128)S(1)} %dynamic-slice_bitcast_fusion.4), kind=kLoop, calls=%fused_computation.5.clone.1 | loop fusion | flops 12578816 | bytes 147456 | tf_op jit(solution)/shard_map/while/body/eval_jaxpr/reduce_sum | solution.py:81
  44.8 5.0 %multiply_reduce_fusion.9 = f32[32,128]{1,0:T(8,128)S(1)} fusion(f32[32,512]{1,0:T(8,128)S(1)} %sqrt_multiply_fusion.4, f32[32,512]{1,0:T(8,128)S(1)} %dynamic-slice_bitcast_fusion.4), kind=kLoop, calls=%fused_computation.5.clone.1 | loop fusion | flops 12578816 | bytes 147456 | tf_op jit(solution)/shard_map/while/body/eval_jaxpr/reduce_sum | solution.py:81
  52.6 13.3 %all-to-all-start = ((f32[64,16,128]{2,1,0:T(8,128)}), f32[64,16,128]{2,1,0:T(8,128)S(1)}, u32[]{:S(2)}, u32[]{:S(2)}) async-start(f32[64,16,128]{2,1,0:T(8,128)} %fusion.72), calls=%async_computation | async-start | bytes 1048576 | tf_op jit(solution)/shard_map/all_to_all | solution.py:17
  65.9 17.7 %all-to-all-done = f32[64,16,128]{2,1,0:T(8,128)S(1)} async-done(((f32[64,16,128]{2,1,0:T(8,128)}), f32[64,16,128]{2,1,0:T(8,128)S(1)}, u32[]{:S(2)}, u32[]{:S(2)}) %all-to-all-start) | async-done | bytes 524320 | tf_op jit(solution)/shard_map/all_to_all | solution.py:17
  89.0 5.7 %all-to-all-start.1 = ((f32[64,16,128]{2,1,0:T(8,128)}), f32[64,16,128]{2,1,0:T(8,128)S(1)}, u32[]{:S(2)}, u32[]{:S(2)}) async-start(f32[64,16,128]{2,1,0:T(8,128)} %broadcast_in_dim.18), calls=%async_computation.1 | async-start | bytes 1048576 | tf_op jit(solution)/shard_map/all_to_all | solution.py:23
  94.7 17.7 %all-to-all-done.1 = f32[64,16,128]{2,1,0:T(8,128)S(1)} async-done(((f32[64,16,128]{2,1,0:T(8,128)}), f32[64,16,128]{2,1,0:T(8,128)S(1)}, u32[]{:S(2)}, u32[]{:S(2)}) %all-to-all-start.1) | async-done | bytes 524320 | tf_op jit(solution)/shard_map/all_to_all | solution.py:23
  113.1 44.0 %while.21 = (s32[]{:T(128)}, f32[8,3,32,512]{3,2,0,1:T(8,128)}, f32[8,3,32,512]{3,2,1,0:T(8,128)S(1)}, f32[8,32,128]{2,1,0:T(8,128)S(1)}, s32[]{:T(128)}) while((s32[]{:T(128)}, f32[8,3,32,512]{3,2,0,1:T(8,128)}, f32[8,3,32,512]{3,2,1,0:T(8,128)S(1)}, f32[8,32,128]{2,1,0:T(8,128)S(1)}, s32[]{:T(128)}) %tuple.47), condition=%wide.region_9.10_spmd, body=%wide.region_6.9_spmd.sunk | while | flops 12713986 | bytes 1032773 | solution.py:99
  113.2 4.7 %multiply_reduce_fusion.11 = f32[32,512]{1,0:T(8,128)S(1)} fusion(f32[32,128]{1,0:T(8,128)S(1)} %dynamic-slice_bitcast_fusion.5, f32[32,512]{1,0:T(8,128)S(1)} %sqrt_multiply_fusion.5), kind=kLoop, calls=%fused_computation.10.clone.1 | loop fusion | flops 12566528 | bytes 147456 | tf_op jit(solution)/shard_map/while/body/eval_jaxpr/reduce_sum | solution.py:96
  118.7 4.7 %multiply_reduce_fusion.11 = f32[32,512]{1,0:T(8,128)S(1)} fusion(f32[32,128]{1,0:T(8,128)S(1)} %dynamic-slice_bitcast_fusion.5, f32[32,512]{1,0:T(8,128)S(1)} %sqrt_multiply_fusion.5), kind=kLoop, calls=%fused_computation.10.clone.1 | loop fusion | flops 12566528 | bytes 147456 | tf_op jit(solution)/shard_map/while/body/eval_jaxpr/reduce_sum | solution.py:96
  124.2 4.7 %multiply_reduce_fusion.11 = f32[32,512]{1,0:T(8,128)S(1)} fusion(f32[32,128]{1,0:T(8,128)S(1)} %dynamic-slice_bitcast_fusion.5, f32[32,512]{1,0:T(8,128)S(1)} %sqrt_multiply_fusion.5), kind=kLoop, calls=%fused_computation.10.clone.1 | loop fusion | flops 12566528 | bytes 147456 | tf_op jit(solution)/shard_map/while/body/eval_jaxpr/reduce_sum | solution.py:96
  129.7 4.7 %multiply_reduce_fusion.11 = f32[32,512]{1,0:T(8,128)S(1)} fusion(f32[32,128]{1,0:T(8,128)S(1)} %dynamic-slice_bitcast_fusion.5, f32[32,512]{1,0:T(8,128)S(1)} %sqrt_multiply_fusion.5), kind=kLoop, calls=%fused_computation.10.clone.1 | loop fusion | flops 12566528 | bytes 147456 | tf_op jit(solution)/shard_map/while/body/eval_jaxpr/reduce_sum | solution.py:96
  135.2 4.7 %multiply_reduce_fusion.11 = f32[32,512]{1,0:T(8,128)S(1)} fusion(f32[32,128]{1,0:T(8,128)S(1)} %dynamic-slice_bitcast_fusion.5, f32[32,512]{1,0:T(8,128)S(1)} %sqrt_multiply_fusion.5), kind=kLoop, calls=%fused_computation.10.clone.1 | loop fusion | flops 12566528 | bytes 147456 | tf_op jit(solution)/shard_map/while/body/eval_jaxpr/reduce_sum | solution.py:96
  140.7 4.7 %multiply_reduce_fusion.11 = f32[32,512]{1,0:T(8,128)S(1)} fusion(f32[32,128]{1,0:T(8,128)S(1)} %dynamic-slice_bitcast_fusion.5, f32[32,512]{1,0:T(8,128)S(1)} %sqrt_multiply_fusion.5), kind=kLoop, calls=%fused_computation.10.clone.1 | loop fusion | flops 12566528 | bytes 147456 | tf_op jit(solution)/shard_map/while/body/eval_jaxpr/reduce_sum | solution.py:96
  146.2 4.7 %multiply_reduce_fusion.11 = f32[32,512]{1,0:T(8,128)S(1)} fusion(f32[32,128]{1,0:T(8,128)S(1)} %dynamic-slice_bitcast_fusion.5, f32[32,512]{1,0:T(8,128)S(1)} %sqrt_multiply_fusion.5), kind=kLoop, calls=%fused_computation.10.clone.1 | loop fusion | flops 12566528 | bytes 147456 | tf_op jit(solution)/shard_map/while/body/eval_jaxpr/reduce_sum | solution.py:96
  151.7 4.7 %multiply_reduce_fusion.11 = f32[32,512]{1,0:T(8,128)S(1)} fusion(f32[32,128]{1,0:T(8,128)S(1)} %dynamic-slice_bitcast_fusion.5, f32[32,512]{1,0:T(8,128)S(1)} %sqrt_multiply_fusion.5), kind=kLoop, calls=%fused_computation.10.clone.1 | loop fusion | flops 12566528 | bytes 147456 | tf_op jit(solution)/shard_map/while/body/eval_jaxpr/reduce_sum | solution.py:96
  157.2 2.1 %convolution_bitcast_fusion = f32[1,3,32,512]{3,2,1,0:T(8,128)S(1)} fusion(f32[3,256,512]{2,1,0:T(8,128)} %bitcast.143, s32[256]{0:T(256)S(1)} %bitcast.175), kind=kOutput, calls=%fused_computation.16 | convolution fusion | flops 151003136 | bytes 1770496 | tf_op jit(solution)/shard_map/dq,vqn->vdn/dot_general | solution.py:105
  159.5 18.0 %all_to_all.15 = f32[4,3,16384]{2,1,0:T(4,128)S(1)} all-to-all(f32[4,3,16384]{2,1,0:T(4,128)S(1)} %broadcast_in_dim.19), channel_id=1, replica_groups=mesh['space'=64,'halo'=4] {'halo'}, dimensions={0} | all-to-all | bytes 1572864 | tf_op jit(solution)/shard_map/all_to_all | solution.py:23
  (136 shorter events, 25.4 us)
Async XLA Ops:
  0.0 1.0 copy-start
  2.8 1.7 copy-start.9
  2.8 1.7 copy-start.5
  7.2 0.8 copy-start.4
  9.0 40.8 %copy-start.1 = (s32[1,1024]{1,0:T(1,128)S(1)}, s32[1,1024]{1,0:T(1,128)}, u32[]{:S(2)}) copy-start(s32[1,1024]{1,0:T(1,128)} %param.19) | copy-start | bytes 12292
  49.8 16.1 %copy-start.8 = (f32[3,128]{1,0:T(4,128)S(1)}, f32[3,128]{1,0:T(4,128)}, u32[]{:S(2)}) copy-start(f32[3,128]{1,0:T(4,128)} %param.22) | copy-start | bytes 4612
  49.8 33.9 %copy-start.2 = (f32[3,128,128]{2,1,0:T(8,128)S(1)}, f32[3,128,128]{2,1,0:T(8,128)}, u32[]{:S(2)}) copy-start(f32[3,128,128]{2,1,0:T(8,128)} %param.21) | copy-start | bytes 589828
  49.8 33.9 %copy-start.3 = (f32[1,16]{1,0:T(1,128)S(1)}, f32[1,16]{1,0:T(1,128)}, u32[]{:S(2)}) copy-start(f32[1,16]{1,0:T(1,128)} %param.20) | copy-start | bytes 196
  52.6 35.5 %copy-start.7 = (f32[3,128]{1,0:T(4,128)S(1)}, f32[3,128]{1,0:T(4,128)}, u32[]{:S(2)}) copy-start(f32[3,128]{1,0:T(4,128)} %param.23) | copy-start | bytes 4612
  52.6 31.0 %all-to-all-start = ((f32[64,16,128]{2,1,0:T(8,128)}), f32[64,16,128]{2,1,0:T(8,128)S(1)}, u32[]{:S(2)}, u32[]{:S(2)}) async-start(f32[64,16,128]{2,1,0:T(8,128)} %fusion.72), calls=%async_computation | async-start | bytes 1048576 | tf_op jit(solution)/shard_map/all_to_all | solution.py:17
  89.0 23.4 %all-to-all-start.1 = ((f32[64,16,128]{2,1,0:T(8,128)}), f32[64,16,128]{2,1,0:T(8,128)S(1)}, u32[]{:S(2)}, u32[]{:S(2)}) async-start(f32[64,16,128]{2,1,0:T(8,128)} %broadcast_in_dim.18), calls=%async_computation.1 | async-start | bytes 1048576 | tf_op jit(solution)/shard_map/all_to_all | solution.py:23
  113.1 44.0 %copy-start.6 = (s32[1,256]{1,0:T(1,128)S(1)}, s32[1,256]{1,0:T(1,128)}, u32[]{:S(2)}) copy-start(s32[1,256]{1,0:T(1,128)} %param.18) | copy-start | bytes 3076
where the time goes:
time: 179 us
  other arithmetic  87.2 us (49%)
  waiting for transfers between devices  35.4 us (20%)
  starting transfers between devices  19 us (11%)
  blocking collectives  18 us (10%)
  local copies, waits for them, and re-layouts  10.1 us (6%)
  matrix products  7.66 us (4%)
    reduce_sum x8, other arithmetic, project(): return jnp.sum(weight_part[:, :, None] * basis, axis=1)  39.8 us
    reduce_sum x8, other arithmetic, evaluate(): scalar = jnp.sum(basis * coef_part[:, None, :], axis=2)  37.7 us
    all_to_all x1, blocking collectives, from_everyone(): return lax.all_to_all(copies, axis, split_axis=0, concat_axis=0, tiled=True)  18 us
    all_to_all x1, waiting for transfers between devices, sum_at_owner(): tiles = lax.all_to_all(split_up(x, dim, length), axis, 0, 0, tiled=True)  17.7 us
    all_to_all x1, waiting for transfers between devices, from_everyone(): return lax.all_to_all(copies, axis, split_axis=0, concat_axis=0, tiled=True)  17.7 us
    all_to_all x1, starting transfers between devices, sum_at_owner(): tiles = lax.all_to_all(split_up(x, dim, length), axis, 0, 0, tiled=True)  13.3 us
    all_to_all x1, starting transfers between devices, from_everyone(): return lax.all_to_all(copies, axis, split_axis=0, concat_axis=0, tiled=True)  5.72 us
    dynamic_update_slice x8, other arithmetic, per_device(): shifted_positions = lax.map(evaluate, (offset_blocks, coef_rows))  5.63 us
  transfers between devices with their start and end apart: 2, of which 2 were waited for; matrix products, arithmetic and copies ran while one was open for 0% of the time, Pallas kernels for 0%

commit v1 on v0

v1 whole, which is shorter than its diff:
```python
import functools

import jax
import jax.numpy as jnp
from jax import lax
from jax.experimental import pallas as pl
from jax.experimental.pallas import tpu as pltpu
from jax.sharding import PartitionSpec as P

BLK = 512
ITERS = 8
KNOTS = 128
TILES = 32
PAIRS = 256
HALOS = 1024
OWNED = 16
CHIPS = 32
GROUPS = 4
ROWS = CHIPS * OWNED
PER_GROUP = ROWS // GROUPS
LANES = 128
QUARTERS = BLK // LANES
SCALE = (KNOTS - 1) / 2.6
F32 = jnp.float32
BF16 = jnp.bfloat16
MESH = pl.DeviceIdType.MESH
VMEM = pl.BlockSpec(memory_space=pltpu.VMEM)


def two_parts(x):
    high = x.astype(BF16)
    return high, (x - high.astype(F32)).astype(BF16)


def three_parts(x):
    high = x.astype(BF16)
    rest = x - high.astype(F32)
    middle = rest.astype(BF16)
    return high, middle, (rest - middle.astype(F32)).astype(BF16)


def one_hot(mask):
    return jnp.where(mask, 1.0, 0.0).astype(BF16)


def matmul(a, b):
    return jnp.dot(a, b, preferred_element_type=F32)


def project_kernel(
    pos, mass, centre, halo, tile, slot, dense, offset, knot, fraction, columns,
    raw, parts, lookup, gathered, left, right, product, pair_rows,
):
    me = lax.axis_index("space")
    core, chip = lax.rem(me, 2), lax.div(me, 2)

    for t in range(TILES):
        for c in range(3):
            raw[t : t + 1, c * BLK : (c + 1) * BLK] = pos[c : c + 1, t * BLK : (t + 1) * BLK]
    for q in range(QUARTERS):
        raw[:, 3 * BLK + q * LANES : 3 * BLK + (q + 1) * LANES] = mass[pl.ds(q, TILES, stride=QUARTERS), :]
    for j, part in enumerate(three_parts(raw[...])):
        parts[j * TILES : (j + 1) * TILES, :] = part
    parts[3 * TILES :, :] = jnp.zeros((TILES, 4 * BLK), BF16)

    owner = slot[...] // OWNED
    half = lax.rem(lax.rem(owner, 2) - core + 2, 2)
    away = lax.rem(lax.div(owner, 2) - chip + CHIPS, CHIPS)
    row = half * ROWS + away * OWNED + lax.rem(slot[...], OWNED)
    lookup[...] = jnp.zeros_like(lookup)
    for j, part in enumerate(three_parts(centre[...])):
        lookup[3 * j : 3 * j + 3, :] = part.astype(F32)
    lookup[9:10, :] = lax.div(row, 32).astype(F32)
    lookup[10:11, :] = lax.rem(row, 32).astype(F32)
    halo_is = one_hot(lax.broadcasted_iota(jnp.int32, (HALOS, PAIRS), 0) == halo[...])
    found = matmul(lookup[...].astype(BF16), halo_is)
    pair_row = found[9:10] * 32.0 + found[10:11]
    by_pair = jnp.concatenate(
        [
            found[0:3] + found[3:6] + found[6:9],
            pair_row,
            tile[...].astype(F32),
            jnp.zeros((LANES - 5, PAIRS), F32),
        ],
        axis=0,
    )
    columns[...] = by_pair.T

    lane = lax.broadcasted_iota(jnp.int32, (PAIRS, LANES), 1)
    tile_is = one_hot(
        (lax.rem(lane, TILES).astype(F32) == columns[:, 4:5]) & (lane < 3 * TILES)
    )
    gathered[...] = matmul(tile_is, parts[...])

    lane8 = lax.broadcasted_iota(jnp.int32, (8, LANES), 1)
    sub8 = lax.broadcasted_iota(jnp.int32, (8, LANES), 0)
    low_lane = lax.rem(lane8, 16)

    def block(b, carry):
        rows = pl.ds(pl.multiple_of(b * 16, 16), 16)
        square = jnp.zeros((16, BLK), F32)
        for c in range(3):
            part = gathered[rows, c * BLK : (c + 1) * BLK] - columns[rows, c : c + 1]
            offset[c, rows, :] = part
            square += part * part
        scaled = jnp.sqrt(square) * SCALE
        below = jnp.floor(scaled)
        rest = scaled - below
        knot[rows, :] = below.astype(jnp.int32)
        fraction[rows, :] = rest
        coarse = jnp.floor(below * 0.125)
        fine = (below - 8.0 * coarse).astype(BF16)
        coarse = coarse.astype(BF16)
        weight = gathered[rows, 3 * BLK :]
        above = weight * rest
        w_below, w_above = two_parts(weight - above), two_parts(above)
        nothing, one = jnp.zeros((16, BLK), BF16), jnp.ones((16, BLK), BF16)
        masks = [fine == jnp.asarray(h, BF16) for h in range(8)]
        for j in range(2):
            for h in range(9):
                value = jnp.where(masks[h - 1], w_above[j], nothing) if h > 0 else nothing
                if h < 8:
                    value = jnp.where(masks[h], w_below[j], value)
                at = (j * 9 + h) * 16
                left[at : at + 16, :] = value
        for j in range(16):
            number = (j % 8) * 2 + j // 8
            right[j * 16 : j * 16 + 16, :] = jnp.where(coarse == jnp.asarray(number, BF16), one, nothing)
        product[...] = lax.dot_general(
            left[...], right[...], (((1,), (1,)), ((), ())), preferred_element_type=F32
        )
        for e in range(2):
            source = (lane8 - low_lane) + sub8 + 8 * e
            total = jnp.zeros((8, LANES), F32)
            for v in range(2):
                for h in range(9):
                    at = h * 16 + 8 * e
                    both = (
                        product[at : at + 8, v * LANES : (v + 1) * LANES]
                        + product[144 + at : 144 + at + 8, v * LANES : (v + 1) * LANES]
                    )
                    own = jnp.take_along_axis(both, source, axis=1)
                    to = 8 * v + h
                    if to == 16:
                        own = pltpu.roll(own, 16, 1)
                    total += jnp.where(low_lane == to % 16, own, 0.0)
            pair_rows[pl.ds(pl.multiple_of(b * 16 + 8 * e, 8), 8), :] = total
        return carry

    lax.fori_loop(0, PAIRS // 16, block, 0)

    row_is = one_hot(
        lax.broadcasted_iota(jnp.int32, (HALOS, PAIRS), 0) == pair_row.astype(jnp.int32)
    )
    both = matmul(row_is, jnp.concatenate(two_parts(pair_rows[...]), axis=1))
    dense[...] = both[:, :KNOTS] + both[:, KNOTS:]


def relax_kernel(
    dense, feedback, mixing, drive, readout, table,
    half_in, sums, sums_in, weights,
    half_send, half_recv, sums_send, sums_recv, coef_send, coef_recv, pass_send, pass_recv,
):
    me = lax.axis_index("space")
    core, chip = lax.rem(me, 2), lax.div(me, 2)
    sibling = {"space": chip * 2 + 1 - core}

    def at_chip(away):
        return {"space": lax.rem(chip + away + CHIPS, CHIPS) * 2 + core}

    barrier = pltpu.get_barrier_semaphore()
    pl.semaphore_signal(barrier, inc=1, device_id=sibling, device_id_type=MESH)
    for d in range(1, CHIPS):
        pl.semaphore_signal(barrier, inc=1, device_id=at_chip(d), device_id_type=MESH)
    for c in range(3):
        high, low = two_parts(mixing[c])
        weights[c, :KNOTS, :KNOTS] = high
        weights[c, KNOTS:, :KNOTS] = high
        weights[c, :KNOTS, KNOTS:] = low
        weights[c, KNOTS:, KNOTS:] = low
    eye = lax.broadcasted_iota(jnp.int32, (OWNED, OWNED), 0) == lax.broadcasted_iota(
        jnp.int32, (OWNED, OWNED), 1
    )
    phi = jnp.sum(jnp.where(eye, feedback[...], 0.0), axis=1, keepdims=True)
    pl.semaphore_wait(barrier, CHIPS)

    halves = []
    for q in range(GROUPS):
        copy = pltpu.make_async_remote_copy(
            src_ref=dense.at[pl.ds(ROWS + q * PER_GROUP, PER_GROUP)],
            dst_ref=half_in.at[pl.ds(q * PER_GROUP, PER_GROUP)],
            send_sem=half_send.at[q],
            recv_sem=half_recv.at[q],
            device_id=sibling,
            device_id_type=MESH,
        )
        copy.start()
        halves.append(copy)
    for q in range(GROUPS):
        halves[q].wait_recv()
        rows = pl.ds(q * PER_GROUP, PER_GROUP)
        sums[rows, :] = dense[rows, :] + half_in[rows, :]
        for d in range(max(1, q * 8), q * 8 + 8):
            pltpu.make_async_remote_copy(
                src_ref=sums.at[pl.ds(d * OWNED, OWNED)],
                dst_ref=sums_in.at[pl.ds((d - 1) * OWNED, OWNED)],
                send_sem=sums_send,
                recv_sem=sums_recv,
                device_id=at_chip(d),
                device_id_type=MESH,
            ).start()
    pltpu.make_async_copy(sums_in, sums_in, sums_recv).wait()
    owned = sums[0:OWNED, :]
    for d in range(1, CHIPS):
        owned += sums_in[(d - 1) * OWNED : d * OWNED, :]

    level = jnp.log1p(owned)
    driven = [drive[c : c + 1, :] * level for c in range(3)]
    state = [jnp.tanh(x) for x in driven]
    for _ in range(ITERS - 1):
        mean = (state[0] + state[1] + state[2]) * (0.5 / 3.0)
        fresh = []
        for c in range(3):
            mixed = matmul(jnp.concatenate(two_parts(state[c]), axis=1), weights[c])
            mixed = mixed[:, :KNOTS] + mixed[:, KNOTS:]
            fresh.append(jnp.tanh(driven[c] + phi * mixed + mean))
        state = fresh
    coef = readout[0:1, :] * state[0] + readout[1:2, :] * state[1] + readout[2:3, :] * state[2]

    table[0:OWNED, :] = coef
    for d in range(1, CHIPS):
        pltpu.make_async_remote_copy(
            src_ref=table.at[pl.ds(0, OWNED)],
            dst_ref=table.at[pl.ds(d * OWNED, OWNED)],
            send_sem=coef_send,
            recv_sem=coef_recv.at[d // 8],
            device_id=at_chip(-d),
            device_id_type=MESH,
        ).start()
    passed = []
    for q in range(GROUPS):
        first = OWNED if q == 0 else q * PER_GROUP
        arrived = table.at[pl.ds(first, (q + 1) * PER_GROUP - first)]
        pltpu.make_async_copy(arrived, arrived, coef_recv.at[q]).wait()
        copy = pltpu.make_async_remote_copy(
            src_ref=table.at[pl.ds(q * PER_GROUP, PER_GROUP)],
            dst_ref=table.at[pl.ds(ROWS + q * PER_GROUP, PER_GROUP)],
            send_sem=pass_send.at[q],
            recv_sem=pass_recv.at[q],
            device_id=sibling,
            device_id_type=MESH,
        )
        copy.start()
        passed.append(copy)
    for copy in passed:
        copy.wait_recv()
    for copy in halves + passed:
        copy.wait_send()
    sent = sums.at[pl.ds(OWNED, ROWS - OWNED)]
    pltpu.make_async_copy(sent, sent, sums_send).wait()
    pltpu.make_async_copy(sent, sent, coef_send).wait()


def evaluate_kernel(table, offset, knot, fraction, columns, tile, shares, coef_rows, moved):
    rows_of = lax.broadcasted_iota(jnp.int32, (PAIRS, HALOS), 1).astype(F32)
    row_is = one_hot(rows_of == columns[:, 3:4])
    both = matmul(row_is, jnp.concatenate(two_parts(table[...]), axis=1))
    coef_rows[...] = both[:, :KNOTS] + both[:, KNOTS:]

    def block(b, carry):
        rows = pl.ds(pl.multiple_of(b * 16, 16), 16)
        coef = coef_rows[rows, :]
        step = pltpu.roll(coef, KNOTS - 1, 1) - coef
        for q in range(QUARTERS):
            lanes = slice(q * LANES, (q + 1) * LANES)
            index = knot[rows, lanes]
            scalar = jnp.take_along_axis(coef, index, axis=1) + fraction[
                rows, lanes
            ] * jnp.take_along_axis(step, index, axis=1)
            for c in range(3):
                high, low = two_parts(offset[c, rows, lanes] * scalar)
                at = (q * 3 + c) * LANES
                moved[rows, at : at + LANES] = high
                moved[rows, 3 * BLK + at : 3 * BLK + at + LANES] = low
        return carry

    lax.fori_loop(0, PAIRS // 16, block, 0)
    tile_is = one_hot(lax.broadcasted_iota(jnp.int32, (TILES, PAIRS), 0) == tile[...])
    for q in range(QUARTERS):
        at = q * 3 * LANES
        share = matmul(tile_is, moved[:, at : at + 3 * LANES]) + matmul(
            tile_is, moved[:, 3 * BLK + at : 3 * BLK + at + 3 * LANES]
        )
        for c in range(3):
            shares[q, c * TILES : (c + 1) * TILES, :] = share[:, c * LANES : (c + 1) * LANES]


def combine_kernel(shares, out, share_in, total_in, total, share_send, share_recv, total_send, total_recv):
    me = lax.axis_index("halo")

    def peer(d):
        return {"halo": lax.rem(me + d + 4, 4)}

    barrier = pltpu.get_barrier_semaphore()
    for d in range(1, 4):
        pl.semaphore_signal(barrier, inc=1, device_id=peer(d), device_id_type=MESH)
    pl.semaphore_wait(barrier, 3)
    copies = []
    for d in (2, 1, 3):
        copy = pltpu.make_async_remote_copy(
            src_ref=shares.at[lax.rem(me + d, 4)],
            dst_ref=share_in.at[d - 1],
            send_sem=share_send.at[d - 1],
            recv_sem=share_recv.at[d - 1],
            device_id=peer(d),
            device_id_type=MESH,
        )
        copy.start()
        copies.append(copy)
    for copy in copies:
        copy.wait_recv()
    total[...] = shares[me] + share_in[0] + share_in[1] + share_in[2]
    for d in (2, 1, 3):
        copy = pltpu.make_async_remote_copy(
            src_ref=total,
            dst_ref=total_in.at[d - 1],
            send_sem=total_send.at[d - 1],
            recv_sem=total_recv.at[d - 1],
            device_id=peer(-d),
            device_id_type=MESH,
        )
        copy.start()
        copies.append(copy)

    def lay_out(block, quarter):
        for t in range(TILES):
            at = pl.ds(pl.multiple_of(t * BLK + quarter * LANES, LANES), LANES)
            for c in range(3):
                out[c : c + 1, at] = block[c * TILES + t : c * TILES + t + 1, :]

    lay_out(total, me)
    for d, copy in zip((2, 1, 3), copies[3:]):
        copy.wait_recv()
        lay_out(total_in.at[d - 1], lax.rem(me + d, 4))
    for copy in copies:
        copy.wait_send()


def call(kernel, outs, scratch, inputs, **params):
    return pl.pallas_call(
        kernel,
        out_shape=outs,
        in_specs=[VMEM] * inputs,
        out_specs=jax.tree.map(lambda _: VMEM, outs),
        scratch_shapes=scratch,
        compiler_params=pltpu.CompilerParams(vmem_limit_bytes=48 * 2**20, **params),
    )


def per_device(
    positions, masses, centres, pair_halo, pair_tile, halo_slot, feedback, mixing, drive, readout
):
    shape = jax.ShapeDtypeStruct
    dma = pltpu.SemaphoreType.DMA
    with jax.named_scope("project"):
        dense, offset, knot, fraction, columns = call(
            project_kernel,
            (
                shape((HALOS, KNOTS), F32),
                shape((3, PAIRS, BLK), F32),
                shape((PAIRS, BLK), jnp.int32),
                shape((PAIRS, BLK), F32),
                shape((PAIRS, LANES), F32),
            ),
            [
                pltpu.VMEM((TILES, 4 * BLK), F32),
                pltpu.VMEM((4 * TILES, 4 * BLK), BF16),
                pltpu.VMEM((16, HALOS), F32),
                pltpu.VMEM((PAIRS, 4 * BLK), F32),
                pltpu.VMEM((18 * 16, BLK), BF16),
                pltpu.VMEM((256, BLK), BF16),
                pltpu.VMEM((18 * 16, 256), F32),
                pltpu.VMEM((PAIRS, KNOTS), F32),
            ],
            6,
        )(
            positions,
            masses.reshape(QUARTERS * TILES, LANES),
            centres[0],
            pair_halo,
            pair_tile,
            halo_slot,
        )
    with jax.named_scope("relax"):
        table = call(
            relax_kernel,
            shape((HALOS, KNOTS), F32),
            [
                pltpu.VMEM((ROWS, KNOTS), F32),
                pltpu.VMEM((ROWS, KNOTS), F32),
                pltpu.VMEM((ROWS - OWNED, KNOTS), F32),
                pltpu.VMEM((3, 2 * KNOTS, 2 * KNOTS), BF16),
                dma((GROUPS,)),
                dma((GROUPS,)),
                dma,
                dma,
                dma,
                dma((GROUPS,)),
                dma((GROUPS,)),
                dma((GROUPS,)),
            ],
            5,
            collective_id=0,
            has_side_effects=True,
        )(dense, feedback, mixing, drive, readout)
    with jax.named_scope("evaluate"):
        shares = call(
            evaluate_kernel,
            shape((QUARTERS, 3 * TILES, LANES), F32),
            [pltpu.VMEM((PAIRS, KNOTS), F32), pltpu.VMEM((PAIRS, 6 * BLK), BF16)],
            6,
        )(table, offset, knot, fraction, columns, pair_tile)
    with jax.named_scope("combine"):
        return call(
            combine_kernel,
            shape((3, TILES * BLK), F32),
            [
                pltpu.VMEM((3, 3 * TILES, LANES), F32),
                pltpu.VMEM((3, 3 * TILES, LANES), F32),
                pltpu.VMEM((3 * TILES, LANES), F32),
                dma((3,)),
                dma((3,)),
                dma((3,)),
                dma((3,)),
            ],
            1,
            collective_id=1,
            has_side_effects=True,
        )(shares)


def solution(mesh):
    return jax.shard_map(
        per_device,
        mesh=mesh,
        in_specs=(
            P(None, "space"),
            P("space"),
            P("halo", None, None),
            P("halo", "space"),
            P("halo", "space"),
            P("halo", None),
            P("halo", "space"),
            P(),
            P(),
            P(),
        ),
        out_specs=P(None, "space"),
        check_vma=False,
    )
```

time: 179 us -> 64.9 us (0.36)
  other arithmetic: 87.2 us -> 0 us
  Pallas kernels: 0 us -> 56.1 us
  waiting for transfers between devices: 35.4 us -> 0 us
  starting transfers between devices: 19 us -> 0 us
  blocking collectives: 18 us -> 0 us
  matrix products: 7.66 us -> 0 us
  local copies, waits for them, and re-layouts: 10.1 us -> 8.19 us
    reduce_sum x35 -> x0, other arithmetic: 78.9 us -> none  [the longest x8 39.8 us: project(): return jnp.sum(weight_part[:, :, None] * basis, axis=1)]
    pallas_call x0 -> x4, Pallas kernels: none -> 56.1 us  [the longest x1 32.7 us: per_device(): call(relax_kernel, shape((HALOS, KNOTS), F32), [pltpu.VMEM((ROWS, KNOTS),...]
    all_to_all x2 -> x0, waiting for transfers between devices: 35.4 us -> none  [the longest x1 17.7 us: sum_at_owner(): tiles = lax.all_to_all(split_up(x, dim, length), axis, 0, 0, tiled=True)]
    all_to_all x2 -> x0, starting transfers between devices: 19 us -> none  [the longest x1 13.3 us: sum_at_owner(): tiles = lax.all_to_all(split_up(x, dim, length), axis, 0, 0, tiled=True)]
    all_to_all x1 -> x0, blocking collectives: 18 us -> none  [from_everyone(): return lax.all_to_all(copies, axis, split_axis=0, concat_axis=0, tiled=True)]
    dot_general x26 -> x0, matrix products: 7.66 us -> none  [the longest x24 4.16 us: relax(): mixed = jnp.dot(state[comp], mixing[comp], precision=lax.Precision.HIGHEST)]
    gather x6 -> x0, local copies, waits for them, and re-layouts: 7.29 us -> none  [the longest x3 4.23 us: per_device(): offsets = places[:, tile_ids, :] - centre_rows[:, halo_ids][:, :, None]]
    unnamed x22 -> x20, local copies, waits for them, and re-layouts: 1.27 us -> 8.19 us
  transfers between devices with their start and end apart: 2 -> 0, of which waited for: 2 -> 0; matrix products, arithmetic and copies ran while one was open for 0% -> 0% of each run, Pallas kernels for 0% -> 0%
where the time goes in v1:
time: 64.9 us; the launch traced here: 64.3 us
  Pallas kernels  56.1 us (86%)
  local copies, waits for them, and re-layouts  8.19 us (13%)
    pallas_call x1, Pallas kernels, per_device(): call(relax_kernel, shape((HALOS, KNOTS), F32), [pltpu.VMEM((ROWS, KNOTS),...  32.7 us
    pallas_call x1, Pallas kernels, per_device(): call(combine_kernel, shape((3, TILES * BLK), F32), [pltpu.VMEM((3, 3 * TI...  10.4 us
    pallas_call x1, Pallas kernels, per_device(): call(project_kernel, (shape((HALOS, KNOTS), F32), shape((3, PAIRS, BLK),...  9.38 us
    unnamed x20, local copies, waits for them, and re-layouts  8.19 us
    pallas_call x1, Pallas kernels, per_device(): call(evaluate_kernel, shape((QUARTERS, 3 * TILES, LANES), F32), [pltpu.VM...  3.66 us

profile of v1, /device:TPU:1, one launch (start us, length us, event | category | flops | bytes accessed | tf_op | source)
XLA Modules:
  0.0 64.3 jit_solution(12574125021330437076)
XLA Ops:
  0.0 0.7 %copy.13 = f32[1,3,1024]{2,1,0:T(4,128)S(1)} copy(f32[1,3,1024]{2,0,1:T(1,128)} %param.12) | data formatting | bytes 24576
  0.7 0.0 copy-start
  0.7 0.9 %copy-done = f32[3,16384]{1,0:T(4,128)S(1)} copy-done((f32[3,16384]{1,0:T(4,128)S(1)}, f32[3,16384]{1,0:T(4,128)}, u32[]{:S(2)}) %copy-start) | copy-done | bytes 196632
  1.7 0.0 copy-start.2
  1.7 0.8 %copy-done.2 = f32[16384]{0:T(1024)S(1)} copy-done((f32[16384]{0:T(1024)S(1)}, f32[16384]{0:T(1024)}, u32[]{:S(2)}) %copy-start.2) | copy-done | bytes 65560
  2.5 0.0 copy-start.3
  2.5 0.7 %copy-done.3 = s32[1,256]{1,0:T(1,128)S(1)} copy-done((s32[1,256]{1,0:T(1,128)S(1)}, s32[1,256]{1,0:T(1,128)}, u32[]{:S(2)}) %copy-start.3) | copy-done | bytes 1048
  3.2 0.0 copy-start.4
  3.2 0.7 %copy-done.4 = s32[1,1024]{1,0:T(1,128)S(1)} copy-done((s32[1,1024]{1,0:T(1,128)S(1)}, s32[1,1024]{1,0:T(1,128)}, u32[]{:S(2)}) %copy-start.4) | copy-done | bytes 4120
  3.9 0.0 copy-start.7
  3.9 0.7 %copy-done.7 = s32[1,256]{1,0:T(1,128)S(1)} copy-done((s32[1,256]{1,0:T(1,128)S(1)}, s32[1,256]{1,0:T(1,128)}, u32[]{:S(2)}) %copy-start.7) | copy-done | bytes 1048
  4.5 9.4 %project.1 = (f32[1024,128]{1,0:T(8,128)S(1)}, f32[3,256,512]{2,1,0:T(8,128)S(1)}, s32[256,512]{1,0:T(8,128)S(1)}, f32[256,512]{1,0:T(8,128)S(1)}, f32[256,128]{1,0:T(8,128)S(1)}) custom-call(f32[3,16384]{1,0:T(4,128)S(1)} %copy-done, f32[128,128]{1,0:T(8,128)S(1)} %bitcast.5, f32[3,1024]{1,0:T(4,128)S(1)} %bitcast.4, s32[1,256]{1,0:T(1,128)S(1)} %copy-done.7, ...), custom_call_target="tpu_custom_call" | custom-call | tf_op jit(solution)/shard_map/project/pallas_call | solution.py:366
  13.9 0.0 copy-start.1
  14.0 0.9 %copy-done.1 = f32[3,128,128]{2,1,0:T(8,128)S(1)} copy-done((f32[3,128,128]{2,1,0:T(8,128)S(1)}, f32[3,128,128]{2,1,0:T(8,128)}, u32[]{:S(2)}) %copy-start.1) | copy-done | bytes 196632
  14.9 0.0 copy-start.5
  14.9 0.7 %copy-done.5 = f32[3,128]{1,0:T(4,128)S(1)} copy-done((f32[3,128]{1,0:T(4,128)S(1)}, f32[3,128]{1,0:T(4,128)}, u32[]{:S(2)}) %copy-start.5) | copy-done | bytes 1560
  15.6 0.0 copy-start.6
  15.6 0.7 %copy-done.6 = f32[3,128]{1,0:T(4,128)S(1)} copy-done((f32[3,128]{1,0:T(4,128)S(1)}, f32[3,128]{1,0:T(4,128)}, u32[]{:S(2)}) %copy-start.6) | copy-done | bytes 1560
  16.2 0.0 copy-start.8
  16.2 0.7 %copy-done.8 = f32[1,16]{1,0:T(1,128)S(1)} copy-done((f32[1,16]{1,0:T(1,128)S(1)}, f32[1,16]{1,0:T(1,128)}, u32[]{:S(2)}) %copy-start.8) | copy-done | bytes 88
  16.9 32.7 %relax.1.table = f32[1024,128]{1,0:T(8,128)S(1)} custom-call(f32[1024,128]{1,0:T(8,128)S(1)} %get-tuple-element.10.dense, f32[1,16]{1,0:T(1,128)S(1)} %copy-done.8, f32[3,128,128]{2,1,0:T(8,128)S(1)} %copy-done.1, f32[3,128]{1,0:T(4,128)S(1)} %copy-done.5, f32[3,128]{1,0:T(4,128)S(1)} %copy-done.6), custom_call_target="tpu_custom_call" | custom-call | tf_op jit(solution)/shard_map/relax/pallas_call | solution.py:395
  49.6 3.7 %evaluate.1.shares = f32[4,96,128]{2,1,0:T(8,128)S(1)} custom-call(f32[1024,128]{1,0:T(8,128)S(1)} %relax.1.table, f32[3,256,512]{2,1,0:T(8,128)S(1)} %get-tuple-element.11.offset, s32[256,512]{1,0:T(8,128)S(1)} %get-tuple-element.12.knot, f32[256,512]{1,0:T(8,128)S(1)} %get-tuple-element.13.fraction, f32[256,128]{1,0:T(8,128)S(1)} %get-tuple-element.14.columns, ...), custom_call_target="tpu_custom_call" | custom-call | tf_op jit(solution)/shard_map/evaluate/pallas_call | solution.py:417
  53.2 10.4 %combine.1 = f32[3,16384]{1,0:T(4,128)S(1)} custom-call(f32[4,96,128]{2,1,0:T(8,128)S(1)} %evaluate.1.shares), custom_call_target="tpu_custom_call" | custom-call | tf_op jit(solution)/shard_map/combine/pallas_call | solution.py:424
  63.6 0.7 %copy.15 = f32[3,16384]{1,0:T(4,128)} copy(f32[3,16384]{1,0:T(4,128)S(1)} %combine.1) | data formatting | bytes 393216
Async XLA Ops:
  0.7 0.9 %copy-start = (f32[3,16384]{1,0:T(4,128)S(1)}, f32[3,16384]{1,0:T(4,128)}, u32[]{:S(2)}) copy-start(f32[3,16384]{1,0:T(4,128)} %pos.1) | copy-start | bytes 589828
  1.7 0.8 %copy-start.2 = (f32[16384]{0:T(1024)S(1)}, f32[16384]{0:T(1024)}, u32[]{:S(2)}) copy-start(f32[16384]{0:T(1024)} %param.11) | copy-start | bytes 196612
  2.5 0.7 %copy-start.3 = (s32[1,256]{1,0:T(1,128)S(1)}, s32[1,256]{1,0:T(1,128)}, u32[]{:S(2)}) copy-start(s32[1,256]{1,0:T(1,128)} %tile.3) | copy-start | bytes 3076
  3.2 0.7 %copy-start.4 = (s32[1,1024]{1,0:T(1,128)S(1)}, s32[1,1024]{1,0:T(1,128)}, u32[]{:S(2)}) copy-start(s32[1,1024]{1,0:T(1,128)} %slot.1) | copy-start | bytes 12292
  3.9 0.7 %copy-start.7 = (s32[1,256]{1,0:T(1,128)S(1)}, s32[1,256]{1,0:T(1,128)}, u32[]{:S(2)}) copy-start(s32[1,256]{1,0:T(1,128)} %halo.1) | copy-start | bytes 3076
  13.9 0.9 %copy-start.1 = (f32[3,128,128]{2,1,0:T(8,128)S(1)}, f32[3,128,128]{2,1,0:T(8,128)}, u32[]{:S(2)}) copy-start(f32[3,128,128]{2,1,0:T(8,128)} %mixing.1) | copy-start | bytes 589828
  14.9 0.7 %copy-start.5 = (f32[3,128]{1,0:T(4,128)S(1)}, f32[3,128]{1,0:T(4,128)}, u32[]{:S(2)}) copy-start(f32[3,128]{1,0:T(4,128)} %drive.1) | copy-start | bytes 4612
  15.6 0.7 %copy-start.6 = (f32[3,128]{1,0:T(4,128)S(1)}, f32[3,128]{1,0:T(4,128)}, u32[]{:S(2)}) copy-start(f32[3,128]{1,0:T(4,128)} %readout.1) | copy-start | bytes 4612
  16.2 0.7 %copy-start.8 = (f32[1,16]{1,0:T(1,128)S(1)}, f32[1,16]{1,0:T(1,128)}, u32[]{:S(2)}) copy-start(f32[1,16]{1,0:T(1,128)} %feedback.1) | copy-start | bytes 196

commit v2 on v0

v2 whole, which is shorter than its diff:
```python
import jax
import jax.numpy as jnp
from jax import lax
from jax.experimental import pallas as pl
from jax.experimental.pallas import tpu as pltpu
from jax.sharding import PartitionSpec as P

BLK = 512
ITERS = 8
KNOTS = 128
TILES = 32
PAIRS = 256
HALOS = 1024
OWNED = 16
N_Y = 4
N_Z = 8
N_X = 4
LINE = N_Z * OWNED
ROWS = N_Y * LINE
LANES = 128
QUARTERS = BLK // LANES
SCALE = (KNOTS - 1) / 2.6
F32 = jnp.float32
BF16 = jnp.bfloat16
MESH = pl.DeviceIdType.MESH


def two_parts(x):
    high = x.astype(BF16)
    return high, (x - high.astype(F32)).astype(BF16)


def three_parts(x):
    high = x.astype(BF16)
    rest = x - high.astype(F32)
    middle = rest.astype(BF16)
    return high, middle, (rest - middle.astype(F32)).astype(BF16)


def one_hot(mask):
    return jnp.where(mask, 1.0, 0.0).astype(BF16)


def matmul(a, b):
    return jnp.dot(a, b, preferred_element_type=F32)


def kernel(
    pos_in, mass_in, centre_in, halo_in, tile_in, slot_in, feedback_in, mixing_in, drive_in, readout_in,
    out,
    pos, mass, centre, halo, tile, slot, feedback, mixing, drive, readout, loaded,
    raw, parts, lookup, gathered, columns, offset, knot, fraction, left, right, product, pair_rows,
    dense, half_in, sums, y_in, z_sums, z_in, weights, table, coef_rows, moved, shares, share_in, total, total_in,
    half_send, half_recv, y_send, y_recv, z_send, z_recv,
    coef_z_send, coef_z_recv, coef_y_send, coef_y_recv, pass_send, pass_recv,
    share_send, share_recv, total_send, total_recv,
):
    inputs = (pos_in, mass_in, centre_in, halo_in, tile_in, slot_in, feedback_in, mixing_in, drive_in, readout_in)
    copies_in = [
        pltpu.make_async_copy(source, target, loaded.at[i])
        for i, (source, target) in enumerate(
            zip(inputs, (pos, mass, centre, halo, tile, slot, feedback, mixing, drive, readout))
        )
    ]
    for copy in copies_in:
        copy.start()

    me = lax.axis_index("space")
    x = lax.axis_index("halo")
    core, y, z = lax.rem(me, 2), lax.rem(lax.div(me, 2), N_Y), lax.div(me, 2 * N_Y)

    def at(dz=0, dy=0, other=0):
        place = lax.rem(z + dz + N_Z, N_Z) * N_Y + lax.rem(y + dy + N_Y, N_Y)
        return {"space": place * 2 + (1 - core if other else core)}

    def beside(d):
        return {"halo": lax.rem(x + d + N_X, N_X)}

    def send(source, target, send_sem, recv_sem, device):
        copy = pltpu.make_async_remote_copy(
            src_ref=source,
            dst_ref=target,
            send_sem=send_sem,
            recv_sem=recv_sem,
            device_id=device,
            device_id_type=MESH,
        )
        copy.start()
        return copy

    def wait_bytes(ref, sem):
        pltpu.make_async_copy(ref, ref, sem).wait()

    barrier = pltpu.get_barrier_semaphore()
    partners = [at(other=1)]
    partners += [at(dy=d) for d in range(1, N_Y)]
    partners += [at(dz=d) for d in range(1, N_Z)]
    partners += [beside(d) for d in range(1, N_X)]
    for partner in partners:
        pl.semaphore_signal(barrier, inc=1, device_id=partner, device_id_type=MESH)

    for i in (2, 3, 4, 5):
        copies_in[i].wait()
    owner = lax.div(slot[...], OWNED)
    half = lax.rem(lax.rem(owner, 2) - core + 2, 2)
    far_y = lax.rem(lax.rem(lax.div(owner, 2), N_Y) - y + N_Y, N_Y)
    far_z = lax.rem(lax.div(owner, 2 * N_Y) - z + N_Z, N_Z)
    row = half * ROWS + far_y * LINE + far_z * OWNED + lax.rem(slot[...], OWNED)
    lookup[...] = jnp.zeros_like(lookup)
    for j, part in enumerate(three_parts(centre[0])):
        lookup[3 * j : 3 * j + 3, :] = part.astype(F32)
    lookup[9:10, :] = lax.div(row, 32).astype(F32)
    lookup[10:11, :] = lax.rem(row, 32).astype(F32)
    halo_is = one_hot(lax.broadcasted_iota(jnp.int32, (HALOS, PAIRS), 0) == halo[...])
    found = matmul(lookup[...].astype(BF16), halo_is)
    pair_row = found[9:10] * 32.0 + found[10:11]
    by_pair = jnp.concatenate(
        [
            found[0:3] + found[3:6] + found[6:9],
            pair_row,
            tile[...].astype(F32),
            jnp.zeros((LANES - 5, PAIRS), F32),
        ],
        axis=0,
    )
    columns[...] = by_pair.T

    for i in (0, 1):
        copies_in[i].wait()
    for t in range(TILES):
        for c in range(3):
            raw[t : t + 1, c * BLK : (c + 1) * BLK] = pos[c : c + 1, t * BLK : (t + 1) * BLK]
    for q in range(QUARTERS):
        raw[:, 3 * BLK + q * LANES : 3 * BLK + (q + 1) * LANES] = mass[pl.ds(q, TILES, stride=QUARTERS), :]
    for j, part in enumerate(three_parts(raw[...])):
        parts[j * TILES : (j + 1) * TILES, :] = part
    parts[3 * TILES :, :] = jnp.zeros((TILES, 4 * BLK), BF16)
    lane = lax.broadcasted_iota(jnp.int32, (PAIRS, LANES), 1)
    tile_is = one_hot((lax.rem(lane, TILES).astype(F32) == columns[:, 4:5]) & (lane < 3 * TILES))
    gathered[...] = matmul(tile_is, parts[...])

    lane8 = lax.broadcasted_iota(jnp.int32, (8, LANES), 1)
    sub8 = lax.broadcasted_iota(jnp.int32, (8, LANES), 0)
    low_lane = lax.rem(lane8, 16)

    def build(start, u):
        rows = pl.ds(pl.multiple_of(start, 16), 16)
        square = jnp.zeros((16, BLK), F32)
        for c in range(3):
            part = gathered[rows, c * BLK : (c + 1) * BLK] - columns[rows, c : c + 1]
            offset[c, rows, :] = part
            square += part * part
        scaled = jnp.sqrt(square) * SCALE
        below = jnp.floor(scaled)
        rest = scaled - below
        knot[rows, :] = below.astype(jnp.int32)
        fraction[rows, :] = rest
        coarse = jnp.floor(below * 0.125)
        fine = (below - 8.0 * coarse).astype(BF16)
        coarse = coarse.astype(BF16)
        weight = gathered[rows, 3 * BLK :]
        above = weight * rest
        w_below, w_above = two_parts(weight - above), two_parts(above)
        nothing, one = jnp.zeros((16, BLK), BF16), jnp.ones((16, BLK), BF16)
        masks = [fine == jnp.asarray(h, BF16) for h in range(8)]
        for j in range(2):
            for h in range(9):
                value = jnp.where(masks[h - 1], w_above[j], nothing) if h > 0 else nothing
                if h < 8:
                    value = jnp.where(masks[h], w_below[j], value)
                spot = (j * 9 + h) * 16
                left[u, spot : spot + 16, :] = value
        for j in range(16):
            number = (j % 8) * 2 + j // 8
            right[u, j * 16 : j * 16 + 16, :] = jnp.where(coarse == jnp.asarray(number, BF16), one, nothing)

    def fold(start, u):
        for e in range(2):
            source = (lane8 - low_lane) + sub8 + 8 * e
            profile = jnp.zeros((8, LANES), F32)
            for v in range(2):
                for h in range(9):
                    spot = h * 16 + 8 * e
                    both = (
                        product[u, spot : spot + 8, v * LANES : (v + 1) * LANES]
                        + product[u, 144 + spot : 144 + spot + 8, v * LANES : (v + 1) * LANES]
                    )
                    own = jnp.take_along_axis(both, source, axis=1)
                    to = 8 * v + h
                    if to == 16:
                        own = pltpu.roll(own, 16, 1)
                    profile += jnp.where(low_lane == to % 16, own, 0.0)
            pair_rows[pl.ds(pl.multiple_of(start + 8 * e, 8), 8), :] = profile

    def block(b, carry):
        for u in range(2):
            build(b * 32 + u * 16, u)
        for u in range(2):
            product[u] = lax.dot_general(
                left[u], right[u], (((1,), (1,)), ((), ())), preferred_element_type=F32
            )
        for u in range(2):
            fold(b * 32 + u * 16, u)
        return carry

    lax.fori_loop(0, PAIRS // 32, block, 0)

    row_is = one_hot(lax.broadcasted_iota(jnp.int32, (HALOS, PAIRS), 0) == pair_row.astype(jnp.int32))
    both = matmul(row_is, jnp.concatenate(two_parts(pair_rows[...]), axis=1))
    dense[...] = both[:, :KNOTS] + both[:, KNOTS:]

    pl.semaphore_wait(barrier, len(partners))
    halves = {}
    for d in (2, 1, 3, 0):
        halves[d] = send(
            dense.at[pl.ds(ROWS + d * LINE, LINE)],
            half_in.at[pl.ds(d * LINE, LINE)],
            half_send.at[d],
            half_recv.at[d],
            at(other=1),
        )
    for i in (6, 7, 8, 9):
        copies_in[i].wait()
    for c in range(3):
        high, low = two_parts(mixing[c])
        weights[c, :KNOTS, :KNOTS] = high
        weights[c, KNOTS:, :KNOTS] = high
        weights[c, :KNOTS, KNOTS:] = low
        weights[c, KNOTS:, KNOTS:] = low
    eye = lax.broadcasted_iota(jnp.int32, (OWNED, OWNED), 0) == lax.broadcasted_iota(
        jnp.int32, (OWNED, OWNED), 1
    )
    phi = jnp.sum(jnp.where(eye, feedback[...], 0.0), axis=1, keepdims=True)

    along_y = []
    for d in (2, 1, 3, 0):
        halves[d].wait_recv()
        rows = pl.ds(d * LINE, LINE)
        sums[rows, :] = dense[rows, :] + half_in[rows, :]
        if d > 0:
            for part in (1, 0):
                along_y.append(
                    send(
                        sums.at[pl.ds(d * LINE + part * LINE // 2, LINE // 2)],
                        y_in.at[pl.ds((d - 1) * LINE + part * LINE // 2, LINE // 2)],
                        y_send.at[part, d - 1],
                        y_recv.at[part, d - 1],
                        at(dy=d),
                    )
                )
    for part in (1, 0):
        for i, d in enumerate((2, 1, 3)):
            along_y[2 * i + (1 - part)].wait_recv()
        first = part * LINE // 2
        rows = pl.ds(first, LINE // 2)
        line = sums[rows, :]
        for d in range(1, N_Y):
            line += y_in[pl.ds((d - 1) * LINE + first, LINE // 2), :]
        z_sums[rows, :] = line
        for d in range(4 * part, 4 * part + 4):
            if d > 0:
                send(
                    z_sums.at[pl.ds(d * OWNED, OWNED)],
                    z_in.at[pl.ds((d - 1) * OWNED, OWNED)],
                    z_send,
                    z_recv,
                    at(dz=d),
                )
    wait_bytes(z_in, z_recv)
    owned = z_sums[0:OWNED, :]
    for d in range(1, N_Z):
        owned += z_in[(d - 1) * OWNED : d * OWNED, :]

    level = jnp.log1p(owned)
    driven = [drive[c : c + 1, :] * level for c in range(3)]
    state = [jnp.tanh(v) for v in driven]
    for _ in range(ITERS - 1):
        mean = (state[0] + state[1] + state[2]) * (0.5 / 3.0)
        fresh = []
        for c in range(3):
            mixed = matmul(jnp.concatenate(two_parts(state[c]), axis=1), weights[c])
            mixed = mixed[:, :KNOTS] + mixed[:, KNOTS:]
            fresh.append(jnp.tanh(driven[c] + phi * mixed + mean))
        state = fresh
    table[0:OWNED, :] = (
        readout[0:1, :] * state[0] + readout[1:2, :] * state[1] + readout[2:3, :] * state[2]
    )

    for d in range(1, N_Z):
        send(
            table.at[pl.ds(0, OWNED)],
            table.at[pl.ds(d * OWNED, OWNED)],
            coef_z_send,
            coef_z_recv.at[d // 4],
            at(dz=-d),
        )
    lines = []
    for part in range(2):
        first = OWNED if part == 0 else LINE // 2
        wait_bytes(table.at[pl.ds(first, (part + 1) * LINE // 2 - first)], coef_z_recv.at[part])
        for d in (2, 1, 3):
            lines.append(
                send(
                    table.at[pl.ds(part * LINE // 2, LINE // 2)],
                    table.at[pl.ds(d * LINE + part * LINE // 2, LINE // 2)],
                    coef_y_send.at[part, d - 1],
                    coef_y_recv.at[part, d - 1],
                    at(dy=-d),
                )
            )
    passed = []
    for d in (0, 1, 3, 2):
        if d > 0:
            for part in range(2):
                lines[3 * part + (2, 1, 3).index(d)].wait_recv()
        passed.append(
            send(
                table.at[pl.ds(d * LINE, LINE)],
                table.at[pl.ds(ROWS + d * LINE, LINE)],
                pass_send.at[d],
                pass_recv.at[d],
                at(other=1),
            )
        )
    for copy in passed:
        copy.wait_recv()

    rows_of = lax.broadcasted_iota(jnp.int32, (PAIRS, HALOS), 1).astype(F32)
    both = matmul(one_hot(rows_of == columns[:, 3:4]), jnp.concatenate(two_parts(table[...]), axis=1))
    coef_rows[...] = both[:, :KNOTS] + both[:, KNOTS:]
    tile_is = one_hot(lax.broadcasted_iota(jnp.int32, (TILES, PAIRS), 0) == tile[...])

    combined = []
    for d in (2, 1, 3, 0):
        lanes = pl.ds(pl.multiple_of(lax.rem(x + d, N_X) * LANES, LANES), LANES)

        def evaluate(b, carry):
            rows = pl.ds(pl.multiple_of(b * 16, 16), 16)
            coef = coef_rows[rows, :]
            step = pltpu.roll(coef, KNOTS - 1, 1) - coef
            index = knot[rows, lanes]
            scalar = jnp.take_along_axis(coef, index, axis=1) + fraction[
                rows, lanes
            ] * jnp.take_along_axis(step, index, axis=1)
            for c in range(3):
                high, low = two_parts(offset[c, rows, lanes] * scalar)
                moved[rows, c * LANES : (c + 1) * LANES] = high
                moved[rows, (c + 3) * LANES : (c + 4) * LANES] = low
            return carry

        lax.fori_loop(0, PAIRS // 16, evaluate, 0, unroll=4)
        share = matmul(tile_is, moved[...])
        for c in range(3):
            shares[d, c * TILES : (c + 1) * TILES, :] = (
                share[:, c * LANES : (c + 1) * LANES] + share[:, (c + 3) * LANES : (c + 4) * LANES]
            )
        if d > 0:
            combined.append(
                send(shares.at[d], share_in.at[d - 1], share_send.at[d - 1], share_recv.at[d - 1], beside(d))
            )
    for copy in combined:
        copy.wait_recv()
    total[...] = shares[0] + share_in[0] + share_in[1] + share_in[2]
    finished = [
        send(total, total_in.at[d - 1], total_send.at[d - 1], total_recv.at[d - 1], beside(-d)) for d in (2, 1, 3)
    ]

    def lay_out(part, quarter):
        for t in range(TILES):
            lanes = pl.ds(pl.multiple_of(t * BLK + quarter * LANES, LANES), LANES)
            for c in range(3):
                out[c : c + 1, lanes] = part[c * TILES + t : c * TILES + t + 1, :]

    lay_out(total, x)
    for d, copy in zip((2, 1, 3), finished):
        copy.wait_recv()
        lay_out(total_in.at[d - 1], lax.rem(x + d, N_X))
    for copy in (*halves.values(), *along_y, *lines, *passed, *combined, *finished):
        copy.wait_send()
    wait_bytes(z_in, z_send)
    wait_bytes(z_in, coef_z_send)


def per_device(
    positions, masses, centres, pair_halo, pair_tile, halo_slot, feedback, mixing, drive, readout
):
    dma = pltpu.SemaphoreType.DMA
    vmem = pltpu.VMEM
    args = (
        positions,
        masses.reshape(QUARTERS * TILES, LANES),
        centres,
        pair_halo,
        pair_tile,
        halo_slot,
        feedback,
        mixing,
        drive,
        readout,
    )
    share = (3 * TILES, LANES)
    return pl.pallas_call(
        kernel,
        out_shape=jax.ShapeDtypeStruct(positions.shape, F32),
        in_specs=[pl.BlockSpec(memory_space=pl.ANY)] * len(args),
        out_specs=pl.BlockSpec(memory_space=vmem),
        scratch_shapes=[
            *(vmem(a.shape, a.dtype) for a in args),
            dma((len(args),)),
            vmem((TILES, 4 * BLK), F32),
            vmem((4 * TILES, 4 * BLK), BF16),
            vmem((16, HALOS), F32),
            vmem((PAIRS, 4 * BLK), F32),
            vmem((PAIRS, LANES), F32),
            vmem((3, PAIRS, BLK), F32),
            vmem((PAIRS, BLK), jnp.int32),
            vmem((PAIRS, BLK), F32),
            vmem((2, 18 * 16, BLK), BF16),
            vmem((2, 256, BLK), BF16),
            vmem((2, 18 * 16, 256), F32),
            vmem((PAIRS, KNOTS), F32),
            vmem((HALOS, KNOTS), F32),
            vmem((ROWS, KNOTS), F32),
            vmem((ROWS, KNOTS), F32),
            vmem((ROWS - LINE, KNOTS), F32),
            vmem((LINE, KNOTS), F32),
            vmem((LINE - OWNED, KNOTS), F32),
            vmem((3, 2 * KNOTS, 2 * KNOTS), BF16),
            vmem((HALOS, KNOTS), F32),
            vmem((PAIRS, KNOTS), F32),
            vmem((PAIRS, 6 * LANES), BF16),
            vmem((N_X, *share), F32),
            vmem((N_X - 1, *share), F32),
            vmem(share, F32),
            vmem((N_X - 1, *share), F32),
            dma((N_Y,)),
            dma((N_Y,)),
            dma((2, N_Y - 1)),
            dma((2, N_Y - 1)),
            dma,
            dma,
            dma,
            dma((2,)),
            dma((2, N_Y - 1)),
            dma((2, N_Y - 1)),
            dma((N_Y,)),
            dma((N_Y,)),
            dma((N_X - 1,)),
            dma((N_X - 1,)),
            dma((N_X - 1,)),
            dma((N_X - 1,)),
        ],
        compiler_params=pltpu.CompilerParams(
            vmem_limit_bytes=48 * 2**20, collective_id=0, has_side_effects=True
        ),
    )(*args)


def solution(mesh):
    return jax.shard_map(
        per_device,
        mesh=mesh,
        in_specs=(
            P(None, "space"),
            P("space"),
            P("halo", None, None),
            P("halo", "space"),
            P("halo", "space"),
            P("halo", None),
            P("halo", "space"),
            P(),
            P(),
            P(),
        ),
        out_specs=P(None, "space"),
        check_vma=False,
    )
```

time: 179 us -> 50.2 us (0.28)
  other arithmetic: 87.2 us -> 0 us
  Pallas kernels: 0 us -> 45.7 us
  waiting for transfers between devices: 35.4 us -> 0 us
  starting transfers between devices: 19 us -> 0 us
  blocking collectives: 18 us -> 0 us
  matrix products: 7.66 us -> 0 us
  local copies, waits for them, and re-layouts: 10.1 us -> 4.21 us
    reduce_sum x35 -> x0, other arithmetic: 78.9 us -> none  [the longest x8 39.8 us: project(): return jnp.sum(weight_part[:, :, None] * basis, axis=1)]
    pallas_call x0 -> x1, Pallas kernels: none -> 45.7 us  [per_device(): pl.pallas_call(kernel, out_shape=jax.ShapeDtypeStruct(positions.shape, F3...]
    all_to_all x2 -> x0, waiting for transfers between devices: 35.4 us -> none  [the longest x1 17.7 us: sum_at_owner(): tiles = lax.all_to_all(split_up(x, dim, length), axis, 0, 0, tiled=True)]
    all_to_all x2 -> x0, starting transfers between devices: 19 us -> none  [the longest x1 13.3 us: sum_at_owner(): tiles = lax.all_to_all(split_up(x, dim, length), axis, 0, 0, tiled=True)]
    all_to_all x1 -> x0, blocking collectives: 18 us -> none  [from_everyone(): return lax.all_to_all(copies, axis, split_axis=0, concat_axis=0, tiled=True)]
    dot_general x26 -> x0, matrix products: 7.66 us -> none  [the longest x24 4.16 us: relax(): mixed = jnp.dot(state[comp], mixing[comp], precision=lax.Precision.HIGHEST)]
    gather x6 -> x0, local copies, waits for them, and re-layouts: 7.29 us -> none  [the longest x3 4.23 us: per_device(): offsets = places[:, tile_ids, :] - centre_rows[:, halo_ids][:, :, None]]
    dynamic_update_slice x8 -> x0, other arithmetic: 5.63 us -> none  [per_device(): shifted_positions = lax.map(evaluate, (offset_blocks, coef_rows))]
  transfers between devices with their start and end apart: 2 -> 0, of which waited for: 2 -> 0; matrix products, arithmetic and copies ran while one was open for 0% -> 0% of each run, Pallas kernels for 0% -> 0%
where the time goes in v2:
time: 50.2 us; the launch traced here: 50 us
  Pallas kernels  45.7 us (91%)
  local copies, waits for them, and re-layouts  4.21 us (8%)
    pallas_call x1, Pallas kernels, per_device(): pl.pallas_call(kernel, out_shape=jax.ShapeDtypeStruct(positions.shape, F3...  45.7 us
    unnamed x20, local copies, waits for them, and re-layouts  4.21 us

profile of v2, /device:TPU:1, one launch (start us, length us, event | category | flops | bytes accessed | tf_op | source)
XLA Modules:
  0.0 50.0 jit_solution(4045999389768359938)
XLA Ops:
  0.0 0.0 copy-start.3
  0.0 0.0 copy-start.4
  0.0 0.0 copy-start.5
  0.0 0.0 copy-start.6
  0.0 0.0 copy-start.7
  0.0 0.0 copy-start.8
  0.0 0.8 %copy.11.centre_in = f32[1,3,1024]{2,1,0:T(4,128)S(1)} copy(f32[1,3,1024]{2,0,1:T(1,128)} %param.12) | data formatting | bytes 24576 | tf_op args[2]
  0.8 0.0 copy-done.3
  0.8 0.0 copy-done.4
  0.8 0.0 copy-done.5
  0.8 0.0 copy-done.6
  0.8 0.0 copy-done.7
  0.8 0.0 copy-done.8
  0.9 0.0 copy-start
  0.9 0.9 %copy-done = f32[3,16384]{1,0:T(4,128)S(1)} copy-done((f32[3,16384]{1,0:T(4,128)S(1)}, f32[3,16384]{1,0:T(4,128)}, u32[]{:S(2)}) %copy-start) | copy-done | bytes 196632
  1.8 0.0 copy-start.1
  1.8 0.9 %copy-done.1 = f32[3,128,128]{2,1,0:T(8,128)S(1)} copy-done((f32[3,128,128]{2,1,0:T(8,128)S(1)}, f32[3,128,128]{2,1,0:T(8,128)}, u32[]{:S(2)}) %copy-start.1) | copy-done | bytes 196632
  2.7 0.0 copy-start.2
  2.7 0.8 %copy-done.2 = f32[16384]{0:T(1024)S(1)} copy-done((f32[16384]{0:T(1024)S(1)}, f32[16384]{0:T(1024)}, u32[]{:S(2)}) %copy-start.2) | copy-done | bytes 65560
  3.6 45.7 %shard_map.100 = f32[3,16384]{1,0:T(4,128)S(1)} custom-call(f32[3,16384]{1,0:T(4,128)S(1)} %copy-done, f32[128,128]{1,0:T(8,128)S(1)} %bitcast.1, f32[1,3,1024]{2,1,0:T(4,128)S(1)} %copy.11.centre_in, s32[1,256]{1,0:T(1,128)S(1)} %copy-done.6, s32[1,256]{1,0:T(1,128)S(1)} %copy-done.7, s32[1,1024]{1,0:T(1,128)S(1)} %copy-done.3, f32[1,16]{1,0:T(1,128)S(1)} %copy-done.8, ...), custom_call_target="tpu_custom_call" | custom-call | tf_op jit(solution)/shard_map/pallas_call | solution.py:402
  49.3 0.7 %copy.13 = f32[3,16384]{1,0:T(4,128)} copy(f32[3,16384]{1,0:T(4,128)S(1)} %shard_map.100) | data formatting | bytes 393216
Async XLA Ops:
  0.0 0.8 %copy-start.3 = (s32[1,1024]{1,0:T(1,128)S(1)}, s32[1,1024]{1,0:T(1,128)}, u32[]{:S(2)}) copy-start(s32[1,1024]{1,0:T(1,128)} %slot_in.1) | copy-start | bytes 12292
  0.0 0.8 %copy-start.4 = (f32[3,128]{1,0:T(4,128)S(1)}, f32[3,128]{1,0:T(4,128)}, u32[]{:S(2)}) copy-start(f32[3,128]{1,0:T(4,128)} %drive_in.1) | copy-start | bytes 4612
  0.0 0.8 %copy-start.5 = (f32[3,128]{1,0:T(4,128)S(1)}, f32[3,128]{1,0:T(4,128)}, u32[]{:S(2)}) copy-start(f32[3,128]{1,0:T(4,128)} %readout_in.1) | copy-start | bytes 4612
  0.0 0.8 %copy-start.6 = (s32[1,256]{1,0:T(1,128)S(1)}, s32[1,256]{1,0:T(1,128)}, u32[]{:S(2)}) copy-start(s32[1,256]{1,0:T(1,128)} %halo_in.1) | copy-start | bytes 3076
  0.0 0.8 %copy-start.7 = (s32[1,256]{1,0:T(1,128)S(1)}, s32[1,256]{1,0:T(1,128)}, u32[]{:S(2)}) copy-start(s32[1,256]{1,0:T(1,128)} %tile_in.1) | copy-start | bytes 3076
  0.0 0.8 %copy-start.8 = (f32[1,16]{1,0:T(1,128)S(1)}, f32[1,16]{1,0:T(1,128)}, u32[]{:S(2)}) copy-start(f32[1,16]{1,0:T(1,128)} %feedback_in.1) | copy-start | bytes 196
  0.9 1.0 %copy-start = (f32[3,16384]{1,0:T(4,128)S(1)}, f32[3,16384]{1,0:T(4,128)}, u32[]{:S(2)}) copy-start(f32[3,16384]{1,0:T(4,128)} %pos_in.1) | copy-start | bytes 589828
  1.8 0.9 %copy-start.1 = (f32[3,128,128]{2,1,0:T(8,128)S(1)}, f32[3,128,128]{2,1,0:T(8,128)}, u32[]{:S(2)}) copy-start(f32[3,128,128]{2,1,0:T(8,128)} %mixing_in.1) | copy-start | bytes 589828
  2.7 0.8 %copy-start.2 = (f32[16384]{0:T(1024)S(1)}, f32[16384]{0:T(1024)}, u32[]{:S(2)}) copy-start(f32[16384]{0:T(1024)} %param.11) | copy-start | bytes 196612

commit v3 on v2

--- a/solution.py
+++ b/solution.py
@@ -15,10 +15,15 @@
 N_Y = 4
 N_Z = 8
 N_X = 4
-LINE = N_Z * OWNED
-ROWS = N_Y * LINE
+PLANE = N_Y * OWNED
+ROWS = N_Z * PLANE
+STEPS = N_Z // 2
+ORDER = (4, 3, 5, 2, 6, 1, 7, 0)
+TURNS = ((7, 1), (6, 1), (4, 2), (2, 2), (0, 2))
+TURNS_OF = (4, 4, 3, 3, 2, 2, 1)
 LANES = 128
 QUARTERS = BLK // LANES
+VMEM_BYTES = 60 * 2**20
 SCALE = (KNOTS - 1) / 2.6
 F32 = jnp.float32
 BF16 = jnp.bfloat16
@@ -105,10 +110,15 @@
     half = lax.rem(lax.rem(owner, 2) - core + 2, 2)
     far_y = lax.rem(lax.rem(lax.div(owner, 2), N_Y) - y + N_Y, N_Y)
     far_z = lax.rem(lax.div(owner, 2 * N_Y) - z + N_Z, N_Z)
-    row = half * ROWS + far_y * LINE + far_z * OWNED + lax.rem(slot[...], OWNED)
+    turn = jnp.where(far_z < N_Z // 2, N_Z - 1 - 2 * far_z, 2 * far_z - N_Z)
+    row = half * ROWS + turn * PLANE + far_y * OWNED + lax.rem(slot[...], OWNED)
     lookup[...] = jnp.zeros_like(lookup)
-    for j, part in enumerate(three_parts(centre[0])):
-        lookup[3 * j : 3 * j + 3, :] = part.astype(F32)
+    for j, part in enumerate(three_parts(centre[...])):
+        part = part.astype(F32)
+        for c in range(3):
+            for i in range(HALOS // LANES):
+                at_row = c * (HALOS // LANES) + i
+                lookup[3 * j + c : 3 * j + c + 1, i * LANES : (i + 1) * LANES] = part[at_row : at_row + 1, :]
     lookup[9:10, :] = lax.div(row, 32).astype(F32)
     lookup[10:11, :] = lax.rem(row, 32).astype(F32)
     halo_is = one_hot(lax.broadcasted_iota(jnp.int32, (HALOS, PAIRS), 0) == halo[...])
@@ -207,18 +217,19 @@
 
     row_is = one_hot(lax.broadcasted_iota(jnp.int32, (HALOS, PAIRS), 0) == pair_row.astype(jnp.int32))
     both = matmul(row_is, jnp.concatenate(two_parts(pair_rows[...]), axis=1))
-    dense[...] = both[:, :KNOTS] + both[:, KNOTS:]
+    dense[...] = (both[:, :KNOTS] + both[:, KNOTS:]).reshape(2 * N_Z, PLANE, KNOTS)
 
     pl.semaphore_wait(barrier, len(partners))
-    halves = {}
-    for d in (2, 1, 3, 0):
-        halves[d] = send(
-            dense.at[pl.ds(ROWS + d * LINE, LINE)],
-            half_in.at[pl.ds(d * LINE, LINE)],
-            half_send.at[d],
-            half_recv.at[d],
+    halves = [
+        send(
+            dense.at[pl.ds(N_Z + 2 * j, 2)],
+            half_in.at[pl.ds(2 * j, 2)],
+            half_send.at[j],
+            half_recv.at[j],
             at(other=1),
         )
+        for j in range(STEPS)
+    ]
     for i in (6, 7, 8, 9):
         copies_in[i].wait()
     for c in range(3):
@@ -232,44 +243,29 @@
     )
     phi = jnp.sum(jnp.where(eye, feedback[...], 0.0), axis=1, keepdims=True)
 
-    along_y = []
-    for d in (2, 1, 3, 0):
-        halves[d].wait_recv()
-        rows = pl.ds(d * LINE, LINE)
-        sums[rows, :] = dense[rows, :] + half_in[rows, :]
-        if d > 0:
-            for part in (1, 0):
-                along_y.append(
-                    send(
-                        sums.at[pl.ds(d * LINE + part * LINE // 2, LINE // 2)],
-                        y_in.at[pl.ds((d - 1) * LINE + part * LINE // 2, LINE // 2)],
-                        y_send.at[part, d - 1],
-                        y_recv.at[part, d - 1],
-                        at(dy=d),
-                    )
-                )
-    for part in (1, 0):
-        for i, d in enumerate((2, 1, 3)):
-            along_y[2 * i + (1 - part)].wait_recv()
-        first = part * LINE // 2
-        rows = pl.ds(first, LINE // 2)
-        line = sums[rows, :]
-        for d in range(1, N_Y):
-            line += y_in[pl.ds((d - 1) * LINE + first, LINE // 2), :]
-        z_sums[rows, :] = line
-        for d in range(4 * part, 4 * part + 4):
-            if d > 0:
-                send(
-                    z_sums.at[pl.ds(d * OWNED, OWNED)],
-                    z_in.at[pl.ds((d - 1) * OWNED, OWNED)],
-                    z_send,
-                    z_recv,
-                    at(dz=d),
-                )
+    for j in range(STEPS):
+        halves[j].wait_recv()
+        turns = pl.ds(2 * j, 2)
+        sums[turns] = dense[turns] + half_in[turns]
+        for d in (2, 1, 3):
+            send(
+                sums.at[turns, pl.ds(d * OWNED, OWNED)],
+                y_in.at[j, d - 1],
+                y_send,
+                y_recv.at[j],
+                at(dy=d),
+            )
+    for j in range(STEPS):
+        wait_bytes(y_in.at[j], y_recv.at[j])
+        plane = sums[2 * j : 2 * j + 2, :OWNED] + y_in[j, 0] + y_in[j, 1] + y_in[j, 2]
+        z_sums[2 * j : 2 * j + 2] = plane
+        for i in (2 * j, 2 * j + 1):
+            if ORDER[i]:
+                send(z_sums.at[i], z_in.at[i], z_send, z_recv, at(dz=ORDER[i]))
     wait_bytes(z_in, z_recv)
-    owned = z_sums[0:OWNED, :]
-    for d in range(1, N_Z):
-        owned += z_in[(d - 1) * OWNED : d * OWNED, :]
+    owned = z_sums[N_Z - 1]
+    for i in range(N_Z - 1):
+        owned += z_in[i]
 
     level = jnp.log1p(owned)
     driven = [drive[c : c + 1, :] * level for c in range(3)]
@@ -282,53 +278,49 @@
             mixed = mixed[:, :KNOTS] + mixed[:, KNOTS:]
             fresh.append(jnp.tanh(driven[c] + phi * mixed + mean))
         state = fresh
-    table[0:OWNED, :] = (
+    table[N_Z - 1, :OWNED] = (
         readout[0:1, :] * state[0] + readout[1:2, :] * state[1] + readout[2:3, :] * state[2]
     )
 
-    for d in range(1, N_Z):
-        send(
-            table.at[pl.ds(0, OWNED)],
-            table.at[pl.ds(d * OWNED, OWNED)],
-            coef_z_send,
-            coef_z_recv.at[d // 4],
-            at(dz=-d),
-        )
-    lines = []
-    for part in range(2):
-        first = OWNED if part == 0 else LINE // 2
-        wait_bytes(table.at[pl.ds(first, (part + 1) * LINE // 2 - first)], coef_z_recv.at[part])
+    own = table.at[N_Z - 1, pl.ds(0, OWNED)]
+    for i in reversed(range(N_Z - 1)):
+        send(own, table.at[i, pl.ds(0, OWNED)], coef_z_send, coef_z_recv.at[TURNS_OF[i]], at(dz=-ORDER[i]))
+    for g, (first, count) in enumerate(TURNS):
+        line = table.at[pl.ds(first, count), pl.ds(0, OWNED)]
+        if g > 0:
+            wait_bytes(line, coef_z_recv.at[g])
         for d in (2, 1, 3):
-            lines.append(
-                send(
-                    table.at[pl.ds(part * LINE // 2, LINE // 2)],
-                    table.at[pl.ds(d * LINE + part * LINE // 2, LINE // 2)],
-                    coef_y_send.at[part, d - 1],
-                    coef_y_recv.at[part, d - 1],
-                    at(dy=-d),
-                )
+            send(
+                line,
+                table.at[pl.ds(first, count), pl.ds(d * OWNED, OWNED)],
+                coef_y_send,
+                coef_y_recv.at[g],
+                at(dy=-d),
             )
     passed = []
-    for d in (0, 1, 3, 2):
-        if d > 0:
-            for part in range(2):
-                lines[3 * part + (2, 1, 3).index(d)].wait_recv()
+    for g, (first, count) in enumerate(TURNS):
+        wait_bytes(table.at[pl.ds(first, count), pl.ds(OWNED, 3 * OWNED)], coef_y_recv.at[g])
         passed.append(
             send(
-                table.at[pl.ds(d * LINE, LINE)],
-                table.at[pl.ds(ROWS + d * LINE, LINE)],
-                pass_send.at[d],
-                pass_recv.at[d],
+                table.at[pl.ds(first, count)],
+                table.at[pl.ds(N_Z + first, count)],
+                pass_send.at[g],
+                pass_recv.at[g],
                 at(other=1),
             )
         )
+
+    def coefficients(first):
+        rows_of = lax.broadcasted_iota(jnp.int32, (PAIRS, ROWS), 1).astype(F32) + first * float(ROWS)
+        rows = table[first * N_Z : (first + 1) * N_Z].reshape(ROWS, KNOTS)
+        both = matmul(one_hot(rows_of == columns[:, 3:4]), jnp.concatenate(two_parts(rows), axis=1))
+        return both[:, :KNOTS] + both[:, KNOTS:]
+
+    coef_rows[...] = coefficients(0)
+    tile_is = one_hot(lax.broadcasted_iota(jnp.int32, (TILES, PAIRS), 0) == tile[...])
     for copy in passed:
         copy.wait_recv()
-
-    rows_of = lax.broadcasted_iota(jnp.int32, (PAIRS, HALOS), 1).astype(F32)
-    both = matmul(one_hot(rows_of == columns[:, 3:4]), jnp.concatenate(two_parts(table[...]), axis=1))
-    coef_rows[...] = both[:, :KNOTS] + both[:, KNOTS:]
-    tile_is = one_hot(lax.broadcasted_iota(jnp.int32, (TILES, PAIRS), 0) == tile[...])
+    coef_rows[...] += coefficients(1)
 
     combined = []
     for d in (2, 1, 3, 0):
@@ -375,8 +367,10 @@
     for d, copy in zip((2, 1, 3), finished):
         copy.wait_recv()
         lay_out(total_in.at[d - 1], lax.rem(x + d, N_X))
-    for copy in (*halves.values(), *along_y, *lines, *passed, *combined, *finished):
+    for copy in (*halves, *passed, *combined, *finished):
         copy.wait_send()
+    wait_bytes(y_in, y_send)
+    wait_bytes(y_in, coef_y_send)
     wait_bytes(z_in, z_send)
     wait_bytes(z_in, coef_z_send)
 
@@ -389,7 +383,7 @@
     args = (
         positions,
         masses.reshape(QUARTERS * TILES, LANES),
-        centres,
+        centres.reshape(3 * HALOS // LANES, LANES),
         pair_halo,
         pair_tile,
         halo_slot,
@@ -419,39 +413,39 @@
             vmem((2, 256, BLK), BF16),
             vmem((2, 18 * 16, 256), F32),
             vmem((PAIRS, KNOTS), F32),
-            vmem((HALOS, KNOTS), F32),
-            vmem((ROWS, KNOTS), F32),
-            vmem((ROWS, KNOTS), F32),
-            vmem((ROWS - LINE, KNOTS), F32),
-            vmem((LINE, KNOTS), F32),
-            vmem((LINE - OWNED, KNOTS), F32),
+            vmem((2 * N_Z, PLANE, KNOTS), F32),
+            vmem((N_Z, PLANE, KNOTS), F32),
+            vmem((N_Z, PLANE, KNOTS), F32),
+            vmem((STEPS, N_Y - 1, 2, OWNED, KNOTS), F32),
+            vmem((N_Z, OWNED, KNOTS), F32),
+            vmem((N_Z - 1, OWNED, KNOTS), F32),
             vmem((3, 2 * KNOTS, 2 * KNOTS), BF16),
-            vmem((HALOS, KNOTS), F32),
+            vmem((2 * N_Z, PLANE, KNOTS), F32),
             vmem((PAIRS, KNOTS), F32),
             vmem((PAIRS, 6 * LANES), BF16),
             vmem((N_X, *share), F32),
             vmem((N_X - 1, *share), F32),
             vmem(share, F32),
             vmem((N_X - 1, *share), F32),
-            dma((N_Y,)),
-            dma((N_Y,)),
-            dma((2, N_Y - 1)),
-            dma((2, N_Y - 1)),
+            dma((STEPS,)),
+            dma((STEPS,)),
+            dma,
+            dma((STEPS,)),
             dma,
             dma,
             dma,
-            dma((2,)),
-            dma((2, N_Y - 1)),
-            dma((2, N_Y - 1)),
-            dma((N_Y,)),
-            dma((N_Y,)),
+            dma((len(TURNS),)),
+            dma,
+            dma((len(TURNS),)),
+            dma((len(TURNS),)),
+            dma((len(TURNS),)),
             dma((N_X - 1,)),
             dma((N_X - 1,)),
             dma((N_X - 1,)),
             dma((N_X - 1,)),
         ],
         compiler_params=pltpu.CompilerParams(
-            vmem_limit_bytes=48 * 2**20, collective_id=0, has_side_effects=True
+            vmem_limit_bytes=VMEM_BYTES, collective_id=0, has_side_effects=True
         ),
     )(*args)
 

time: 50.2 us -> 46.8 us (0.932)
  local copies, waits for them, and re-layouts: 4.21 us -> 1.7 us
  Pallas kernels: 45.7 us -> 45 us
    unnamed x20 -> x1, local copies, waits for them, and re-layouts: 4.21 us -> 1.7 us
    pallas_call x1, Pallas kernels: 45.7 us -> 45 us  [per_device(): pl.pallas_call(kernel, out_shape=jax.ShapeDtypeStruct(positions.shape, F3...]
where the time goes in v3:
time: 46.8 us; the launch traced here: 46.7 us
  Pallas kernels  45 us (96%)
  local copies, waits for them, and re-layouts  1.7 us (4%)
    pallas_call x1, Pallas kernels, per_device(): pl.pallas_call(kernel, out_shape=jax.ShapeDtypeStruct(positions.shape, F3...  45 us
    unnamed x1, local copies, waits for them, and re-layouts  1.7 us

profile of v3, /device:TPU:1, one launch (start us, length us, event | category | flops | bytes accessed | tf_op | source)
XLA Modules:
  0.0 46.7 jit_solution(13180426280571724065)
XLA Ops:
  0.0 45.0 %shard_map.100 = f32[3,16384]{1,0:T(4,128)} custom-call(f32[3,16384]{1,0:T(4,128)} %pos_in.1, f32[128,128]{1,0:T(8,128)} %bitcast.2, f32[24,128]{1,0:T(8,128)} %bitcast.3, s32[1,256]{1,0:T(1,128)} %halo_in.1, s32[1,256]{1,0:T(1,128)} %tile_in.1, s32[1,1024]{1,0:T(1,128)} %slot_in.1, f32[1,16]{1,0:T(1,128)} %feedback_in.1, f32[3,128,128]{2,1,0:T(8,128)} %mixing_in.1, ...), custom_call_target="tpu_custom_call" | custom-call | tf_op jit(solution)/shard_map/pallas_call | solution.py:396
  45.0 1.7 %copy.12 = f32[3,16384]{1,0:T(4,128)} copy(f32[3,16384]{1,0:T(4,128)} %shard_map.100) | data formatting | bytes 393216

commit v4 on v3

--- a/solution.py
+++ b/solution.py
@@ -21,6 +21,7 @@
 ORDER = (4, 3, 5, 2, 6, 1, 7, 0)
 TURNS = ((7, 1), (6, 1), (4, 2), (2, 2), (0, 2))
 TURNS_OF = (4, 4, 3, 3, 2, 2, 1)
+PASSED = 3
 LANES = 128
 QUARTERS = BLK // LANES
 VMEM_BYTES = 60 * 2**20
@@ -57,7 +58,7 @@
     raw, parts, lookup, gathered, columns, offset, knot, fraction, left, right, product, pair_rows,
     dense, half_in, sums, y_in, z_sums, z_in, weights, table, coef_rows, moved, shares, share_in, total, total_in,
     half_send, half_recv, y_send, y_recv, z_send, z_recv,
-    coef_z_send, coef_z_recv, coef_y_send, coef_y_recv, pass_send, pass_recv,
+    coef_z_send, coef_z_recv, coef_y_send, coef_y_recv, coef_both_send, coef_both_recv, pass_send, pass_recv,
     share_send, share_recv, total_send, total_recv,
 ):
     inputs = (pos_in, mass_in, centre_in, halo_in, tile_in, slot_in, feedback_in, mixing_in, drive_in, readout_in)
@@ -213,7 +214,7 @@
             fold(b * 32 + u * 16, u)
         return carry
 
-    lax.fori_loop(0, PAIRS // 32, block, 0)
+    lax.fori_loop(0, PAIRS // 32, block, 0, unroll=8)
 
     row_is = one_hot(lax.broadcasted_iota(jnp.int32, (HALOS, PAIRS), 0) == pair_row.astype(jnp.int32))
     both = matmul(row_is, jnp.concatenate(two_parts(pair_rows[...]), axis=1))
@@ -285,6 +286,7 @@
     own = table.at[N_Z - 1, pl.ds(0, OWNED)]
     for i in reversed(range(N_Z - 1)):
         send(own, table.at[i, pl.ds(0, OWNED)], coef_z_send, coef_z_recv.at[TURNS_OF[i]], at(dz=-ORDER[i]))
+    passed = []
     for g, (first, count) in enumerate(TURNS):
         line = table.at[pl.ds(first, count), pl.ds(0, OWNED)]
         if g > 0:
@@ -297,18 +299,36 @@
                 coef_y_recv.at[g],
                 at(dy=-d),
             )
-    passed = []
+        if g >= PASSED:
+            for d in (2, 1, 3):
+                send(
+                    line,
+                    table.at[pl.ds(N_Z + first, count), pl.ds(d * OWNED, OWNED)],
+                    coef_both_send,
+                    coef_both_recv.at[g - PASSED],
+                    at(dy=-d, other=1),
+                )
+            passed.append(
+                send(
+                    line,
+                    table.at[pl.ds(N_Z + first, count), pl.ds(0, OWNED)],
+                    pass_send.at[g],
+                    pass_recv.at[g],
+                    at(other=1),
+                )
+            )
     for g, (first, count) in enumerate(TURNS):
         wait_bytes(table.at[pl.ds(first, count), pl.ds(OWNED, 3 * OWNED)], coef_y_recv.at[g])
-        passed.append(
-            send(
-                table.at[pl.ds(first, count)],
-                table.at[pl.ds(N_Z + first, count)],
-                pass_send.at[g],
-                pass_recv.at[g],
-                at(other=1),
-            )
-        )
+        if g < PASSED:
+            passed.append(
+                send(
+                    table.at[pl.ds(first, count)],
+                    table.at[pl.ds(N_Z + first, count)],
+                    pass_send.at[g],
+                    pass_recv.at[g],
+                    at(other=1),
+                )
+            )
 
     def coefficients(first):
         rows_of = lax.broadcasted_iota(jnp.int32, (PAIRS, ROWS), 1).astype(F32) + first * float(ROWS)
@@ -320,6 +340,8 @@
     tile_is = one_hot(lax.broadcasted_iota(jnp.int32, (TILES, PAIRS), 0) == tile[...])
     for copy in passed:
         copy.wait_recv()
+    for g, (first, count) in enumerate(TURNS[PASSED:]):
+        wait_bytes(table.at[pl.ds(N_Z + first, count), pl.ds(OWNED, 3 * OWNED)], coef_both_recv.at[g])
     coef_rows[...] += coefficients(1)
 
     combined = []
@@ -371,6 +393,7 @@
         copy.wait_send()
     wait_bytes(y_in, y_send)
     wait_bytes(y_in, coef_y_send)
+    wait_bytes(table.at[pl.ds(0, 4), pl.ds(OWNED, 3 * OWNED)], coef_both_send)
     wait_bytes(z_in, z_send)
     wait_bytes(z_in, coef_z_send)
 
@@ -437,6 +460,8 @@
             dma((len(TURNS),)),
             dma,
             dma((len(TURNS),)),
+            dma,
+            dma((len(TURNS) - PASSED,)),
             dma((len(TURNS),)),
             dma((len(TURNS),)),
             dma((N_X - 1,)),

time: 46.8 us -> 43.1 us (0.921)
  Pallas kernels: 45 us -> 41.3 us
    pallas_call x1, Pallas kernels: 45 us -> 41.3 us  [per_device(): pl.pallas_call(kernel, out_shape=jax.ShapeDtypeStruct(positions.shape, F3...]
where the time goes in v4:
time: 43.1 us; the launch traced here: 43 us
  Pallas kernels  41.3 us (96%)
  local copies, waits for them, and re-layouts  1.7 us (4%)
    pallas_call x1, Pallas kernels, per_device(): pl.pallas_call(kernel, out_shape=jax.ShapeDtypeStruct(positions.shape, F3...  41.3 us
    unnamed x1, local copies, waits for them, and re-layouts  1.7 us

profile of v4, /device:TPU:1, one launch (start us, length us, event | category | flops | bytes accessed | tf_op | source)
XLA Modules:
  0.0 43.0 jit_solution(3862404273674936346)
XLA Ops:
  0.0 41.3 %shard_map.100 = f32[3,16384]{1,0:T(4,128)} custom-call(f32[3,16384]{1,0:T(4,128)} %pos_in.1, f32[128,128]{1,0:T(8,128)} %bitcast.2, f32[24,128]{1,0:T(8,128)} %bitcast.3, s32[1,256]{1,0:T(1,128)} %halo_in.1, s32[1,256]{1,0:T(1,128)} %tile_in.1, s32[1,1024]{1,0:T(1,128)} %slot_in.1, f32[1,16]{1,0:T(1,128)} %feedback_in.1, f32[3,128,128]{2,1,0:T(8,128)} %mixing_in.1, ...), custom_call_target="tpu_custom_call" | custom-call | tf_op jit(solution)/shard_map/pallas_call | solution.py:419
  41.3 1.7 %copy.12 = f32[3,16384]{1,0:T(4,128)} copy(f32[3,16384]{1,0:T(4,128)} %shard_map.100) | data formatting | bytes 393216

commit v5 on v4

--- a/solution.py
+++ b/solution.py
@@ -22,8 +22,11 @@
 TURNS = ((7, 1), (6, 1), (4, 2), (2, 2), (0, 2))
 TURNS_OF = (4, 4, 3, 3, 2, 2, 1)
 PASSED = 3
+DIRECT = 1
 LANES = 128
 QUARTERS = BLK // LANES
+PARTS = 2
+PART = 3 * TILES // PARTS
 VMEM_BYTES = 60 * 2**20
 SCALE = (KNOTS - 1) / 2.6
 F32 = jnp.float32
@@ -56,8 +59,8 @@
     out,
     pos, mass, centre, halo, tile, slot, feedback, mixing, drive, readout, loaded,
     raw, parts, lookup, gathered, columns, offset, knot, fraction, left, right, product, pair_rows,
-    dense, half_in, sums, y_in, z_sums, z_in, weights, table, coef_rows, moved, shares, share_in, total, total_in,
-    half_send, half_recv, y_send, y_recv, z_send, z_recv,
+    dense, half_in, sums, y_in, y_other, z_sums, z_in, weights, table, coef_rows, moved, shares, share_in, total, total_in,
+    half_send, half_recv, y_send, y_recv, other_send, other_recv, z_send, z_recv,
     coef_z_send, coef_z_recv, coef_y_send, coef_y_recv, coef_both_send, coef_both_recv, pass_send, pass_recv,
     share_send, share_recv, total_send, total_recv,
 ):
@@ -99,13 +102,13 @@
 
     barrier = pltpu.get_barrier_semaphore()
     partners = [at(other=1)]
-    partners += [at(dy=d) for d in range(1, N_Y)]
+    partners += [at(dy=d, other=o) for d in range(1, N_Y) for o in range(2)]
     partners += [at(dz=d) for d in range(1, N_Z)]
     partners += [beside(d) for d in range(1, N_X)]
     for partner in partners:
         pl.semaphore_signal(barrier, inc=1, device_id=partner, device_id_type=MESH)
 
-    for i in (2, 3, 4, 5):
+    for i in range(6):
         copies_in[i].wait()
     owner = lax.div(slot[...], OWNED)
     half = lax.rem(lax.rem(owner, 2) - core + 2, 2)
@@ -136,8 +139,6 @@
     )
     columns[...] = by_pair.T
 
-    for i in (0, 1):
-        copies_in[i].wait()
     for t in range(TILES):
         for c in range(3):
             raw[t : t + 1, c * BLK : (c + 1) * BLK] = pos[c : c + 1, t * BLK : (t + 1) * BLK]
@@ -216,21 +217,42 @@
 
     lax.fori_loop(0, PAIRS // 32, block, 0, unroll=8)
 
-    row_is = one_hot(lax.broadcasted_iota(jnp.int32, (HALOS, PAIRS), 0) == pair_row.astype(jnp.int32))
-    both = matmul(row_is, jnp.concatenate(two_parts(pair_rows[...]), axis=1))
-    dense[...] = (both[:, :KNOTS] + both[:, KNOTS:]).reshape(2 * N_Z, PLANE, KNOTS)
+    profiles = jnp.concatenate(two_parts(pair_rows[...]), axis=1)
+
+    def sum_rows(first, count):
+        rows_of = lax.broadcasted_iota(jnp.int32, (count * PLANE, PAIRS), 0) + first * PLANE
+        both = matmul(one_hot(rows_of == pair_row.astype(jnp.int32)), profiles)
+        dense[first : first + count] = (both[:, :KNOTS] + both[:, KNOTS:]).reshape(count, PLANE, KNOTS)
+
+    sum_rows(0, 2 * DIRECT)
+    sum_rows(N_Z, 2 * DIRECT)
 
     pl.semaphore_wait(barrier, len(partners))
-    halves = [
-        send(
-            dense.at[pl.ds(N_Z + 2 * j, 2)],
-            half_in.at[pl.ds(2 * j, 2)],
-            half_send.at[j],
-            half_recv.at[j],
-            at(other=1),
+    for j in range(DIRECT):
+        for d in (2, 1, 3):
+            rows = pl.ds(d * OWNED, OWNED)
+            send(dense.at[pl.ds(2 * j, 2), rows], y_in.at[j, d - 1], y_send, y_recv.at[j], at(dy=d))
+            send(
+                dense.at[pl.ds(N_Z + 2 * j, 2), rows],
+                y_other.at[j, d - 1],
+                other_send,
+                other_recv.at[j],
+                at(dy=d, other=1),
+            )
+    sum_rows(N_Z + 2 * DIRECT, N_Z - 2 * DIRECT)
+    halves = []
+    for j in range(STEPS):
+        rows = pl.ds(0, OWNED if j < DIRECT else PLANE)
+        halves.append(
+            send(
+                dense.at[pl.ds(N_Z + 2 * j, 2), rows],
+                half_in.at[pl.ds(2 * j, 2), rows],
+                half_send.at[j],
+                half_recv.at[j],
+                at(other=1),
+            )
         )
-        for j in range(STEPS)
-    ]
+    sum_rows(2 * DIRECT, N_Z - 2 * DIRECT)
     for i in (6, 7, 8, 9):
         copies_in[i].wait()
     for c in range(3):
@@ -244,7 +266,7 @@
     )
     phi = jnp.sum(jnp.where(eye, feedback[...], 0.0), axis=1, keepdims=True)
 
-    for j in range(STEPS):
+    for j in range(DIRECT, STEPS):
         halves[j].wait_recv()
         turns = pl.ds(2 * j, 2)
         sums[turns] = dense[turns] + half_in[turns]
@@ -257,8 +279,15 @@
                 at(dy=d),
             )
     for j in range(STEPS):
+        turns = slice(2 * j, 2 * j + 2)
+        if j < DIRECT:
+            halves[j].wait_recv()
+            wait_bytes(y_other.at[j], other_recv.at[j])
+            plane = dense[turns, :OWNED] + half_in[turns, :OWNED] + y_other[j, 0] + y_other[j, 1] + y_other[j, 2]
+        else:
+            plane = sums[turns, :OWNED]
         wait_bytes(y_in.at[j], y_recv.at[j])
-        plane = sums[2 * j : 2 * j + 2, :OWNED] + y_in[j, 0] + y_in[j, 1] + y_in[j, 2]
+        plane += y_in[j, 0] + y_in[j, 1] + y_in[j, 2]
         z_sums[2 * j : 2 * j + 2] = plane
         for i in (2 * j, 2 * j + 1):
             if ORDER[i]:
@@ -362,22 +391,40 @@
                 moved[rows, (c + 3) * LANES : (c + 4) * LANES] = low
             return carry
 
-        lax.fori_loop(0, PAIRS // 16, evaluate, 0, unroll=4)
+        lax.fori_loop(0, PAIRS // 16, evaluate, 0, unroll=8)
         share = matmul(tile_is, moved[...])
         for c in range(3):
             shares[d, c * TILES : (c + 1) * TILES, :] = (
                 share[:, c * LANES : (c + 1) * LANES] + share[:, (c + 3) * LANES : (c + 4) * LANES]
             )
         if d > 0:
-            combined.append(
-                send(shares.at[d], share_in.at[d - 1], share_send.at[d - 1], share_recv.at[d - 1], beside(d))
-            )
-    for copy in combined:
-        copy.wait_recv()
-    total[...] = shares[0] + share_in[0] + share_in[1] + share_in[2]
-    finished = [
-        send(total, total_in.at[d - 1], total_send.at[d - 1], total_recv.at[d - 1], beside(-d)) for d in (2, 1, 3)
-    ]
+            for part in range(PARTS):
+                rows = pl.ds(part * PART, PART)
+                combined.append(
+                    send(
+                        shares.at[d, rows],
+                        share_in.at[d - 1, rows],
+                        share_send.at[part, d - 1],
+                        share_recv.at[part, d - 1],
+                        beside(d),
+                    )
+                )
+    finished = []
+    for part in range(PARTS):
+        for copy in combined[part::PARTS]:
+            copy.wait_recv()
+        rows = pl.ds(part * PART, PART)
+        total[rows, :] = shares[0, rows] + share_in[0, rows] + share_in[1, rows] + share_in[2, rows]
+        for d in (2, 1, 3):
+            finished.append(
+                send(
+                    total.at[rows],
+                    total_in.at[d - 1, rows],
+                    total_send.at[part, d - 1],
+                    total_recv.at[part, d - 1],
+                    beside(-d),
+                )
+            )
 
     def lay_out(part, quarter):
         for t in range(TILES):
@@ -386,12 +433,14 @@
                 out[c : c + 1, lanes] = part[c * TILES + t : c * TILES + t + 1, :]
 
     lay_out(total, x)
-    for d, copy in zip((2, 1, 3), finished):
-        copy.wait_recv()
+    for i, d in ((1, 1), (2, 3), (0, 2)):
+        for part in range(PARTS):
+            finished[3 * part + i].wait_recv()
         lay_out(total_in.at[d - 1], lax.rem(x + d, N_X))
     for copy in (*halves, *passed, *combined, *finished):
         copy.wait_send()
     wait_bytes(y_in, y_send)
+    wait_bytes(y_other, other_send)
     wait_bytes(y_in, coef_y_send)
     wait_bytes(table.at[pl.ds(0, 4), pl.ds(OWNED, 3 * OWNED)], coef_both_send)
     wait_bytes(z_in, z_send)
@@ -440,6 +489,7 @@
             vmem((N_Z, PLANE, KNOTS), F32),
             vmem((N_Z, PLANE, KNOTS), F32),
             vmem((STEPS, N_Y - 1, 2, OWNED, KNOTS), F32),
+            vmem((DIRECT, N_Y - 1, 2, OWNED, KNOTS), F32),
             vmem((N_Z, OWNED, KNOTS), F32),
             vmem((N_Z - 1, OWNED, KNOTS), F32),
             vmem((3, 2 * KNOTS, 2 * KNOTS), BF16),
@@ -455,6 +505,8 @@
             dma,
             dma((STEPS,)),
             dma,
+            dma((DIRECT,)),
+            dma,
             dma,
             dma,
             dma((len(TURNS),)),
@@ -464,10 +516,10 @@
             dma((len(TURNS) - PASSED,)),
             dma((len(TURNS),)),
             dma((len(TURNS),)),
-            dma((N_X - 1,)),
-            dma((N_X - 1,)),
-            dma((N_X - 1,)),
-            dma((N_X - 1,)),
+            dma((PARTS, N_X - 1)),
+            dma((PARTS, N_X - 1)),
+            dma((PARTS, N_X - 1)),
+            dma((PARTS, N_X - 1)),
         ],
         compiler_params=pltpu.CompilerParams(
             vmem_limit_bytes=VMEM_BYTES, collective_id=0, has_side_effects=True

time: 43.1 us -> 41.2 us (0.956)
  Pallas kernels: 41.3 us -> 39.4 us
    pallas_call x1, Pallas kernels: 41.3 us -> 39.4 us  [per_device(): pl.pallas_call(kernel, out_shape=jax.ShapeDtypeStruct(positions.shape, F3...]
where the time goes in v5:
time: 41.2 us; the launch traced here: 41.1 us
  Pallas kernels  39.4 us (96%)
  local copies, waits for them, and re-layouts  1.7 us (4%)
    pallas_call x1, Pallas kernels, per_device(): pl.pallas_call(kernel, out_shape=jax.ShapeDtypeStruct(positions.shape, F3...  39.4 us
    unnamed x1, local copies, waits for them, and re-layouts  1.7 us

profile of v5, /device:TPU:1, one launch (start us, length us, event | category | flops | bytes accessed | tf_op | source)
XLA Modules:
  0.0 41.1 jit_solution(17303242759026550630)
XLA Ops:
  0.0 39.4 %shard_map.100 = f32[3,16384]{1,0:T(4,128)} custom-call(f32[3,16384]{1,0:T(4,128)} %pos_in.1, f32[128,128]{1,0:T(8,128)} %bitcast.2, f32[24,128]{1,0:T(8,128)} %bitcast.3, s32[1,256]{1,0:T(1,128)} %halo_in.1, s32[1,256]{1,0:T(1,128)} %tile_in.1, s32[1,1024]{1,0:T(1,128)} %slot_in.1, f32[1,16]{1,0:T(1,128)} %feedback_in.1, f32[3,128,128]{2,1,0:T(8,128)} %mixing_in.1, ...), custom_call_target="tpu_custom_call" | custom-call | tf_op jit(solution)/shard_map/pallas_call | solution.py:468
  39.4 1.7 %copy.12 = f32[3,16384]{1,0:T(4,128)} copy(f32[3,16384]{1,0:T(4,128)} %shard_map.100) | data formatting | bytes 393216

commit v6 on v5

--- a/solution.py
+++ b/solution.py
@@ -59,7 +59,7 @@
     out,
     pos, mass, centre, halo, tile, slot, feedback, mixing, drive, readout, loaded,
     raw, parts, lookup, gathered, columns, offset, knot, fraction, left, right, product, pair_rows,
-    dense, half_in, sums, y_in, y_other, z_sums, z_in, weights, table, coef_rows, moved, shares, share_in, total, total_in,
+    dense, half_in, sums, y_in, y_other, z_sums, z_in, weights, table, picked, tile_of, coef_rows, moved, shares, share_in, total, total_in,
     half_send, half_recv, y_send, y_recv, other_send, other_recv, z_send, z_recv,
     coef_z_send, coef_z_recv, coef_y_send, coef_y_recv, coef_both_send, coef_both_recv, pass_send, pass_recv,
     share_send, share_recv, total_send, total_recv,
@@ -266,6 +266,11 @@
     )
     phi = jnp.sum(jnp.where(eye, feedback[...], 0.0), axis=1, keepdims=True)
 
+    rows_of = lax.broadcasted_iota(jnp.int32, (PAIRS, ROWS), 1).astype(F32)
+    for first in range(2):
+        picked[first] = one_hot(rows_of + first * float(ROWS) == columns[:, 3:4])
+    tile_of[...] = one_hot(lax.broadcasted_iota(jnp.int32, (TILES, PAIRS), 0) == tile[...])
+
     for j in range(DIRECT, STEPS):
         halves[j].wait_recv()
         turns = pl.ds(2 * j, 2)
@@ -313,7 +318,7 @@
     )
 
     own = table.at[N_Z - 1, pl.ds(0, OWNED)]
-    for i in reversed(range(N_Z - 1)):
+    for i in range(N_Z - 1):
         send(own, table.at[i, pl.ds(0, OWNED)], coef_z_send, coef_z_recv.at[TURNS_OF[i]], at(dz=-ORDER[i]))
     passed = []
     for g, (first, count) in enumerate(TURNS):
@@ -360,13 +365,11 @@
             )
 
     def coefficients(first):
-        rows_of = lax.broadcasted_iota(jnp.int32, (PAIRS, ROWS), 1).astype(F32) + first * float(ROWS)
         rows = table[first * N_Z : (first + 1) * N_Z].reshape(ROWS, KNOTS)
-        both = matmul(one_hot(rows_of == columns[:, 3:4]), jnp.concatenate(two_parts(rows), axis=1))
+        both = matmul(picked[first], jnp.concatenate(two_parts(rows), axis=1))
         return both[:, :KNOTS] + both[:, KNOTS:]
 
     coef_rows[...] = coefficients(0)
-    tile_is = one_hot(lax.broadcasted_iota(jnp.int32, (TILES, PAIRS), 0) == tile[...])
     for copy in passed:
         copy.wait_recv()
     for g, (first, count) in enumerate(TURNS[PASSED:]):
@@ -391,8 +394,8 @@
                 moved[rows, (c + 3) * LANES : (c + 4) * LANES] = low
             return carry
 
-        lax.fori_loop(0, PAIRS // 16, evaluate, 0, unroll=8)
-        share = matmul(tile_is, moved[...])
+        lax.fori_loop(0, PAIRS // 16, evaluate, 0, unroll=16)
+        share = matmul(tile_of[...], moved[...])
         for c in range(3):
             shares[d, c * TILES : (c + 1) * TILES, :] = (
                 share[:, c * LANES : (c + 1) * LANES] + share[:, (c + 3) * LANES : (c + 4) * LANES]
@@ -494,6 +497,8 @@
             vmem((N_Z - 1, OWNED, KNOTS), F32),
             vmem((3, 2 * KNOTS, 2 * KNOTS), BF16),
             vmem((2 * N_Z, PLANE, KNOTS), F32),
+            vmem((2, PAIRS, ROWS), BF16),
+            vmem((TILES, PAIRS), BF16),
             vmem((PAIRS, KNOTS), F32),
             vmem((PAIRS, 6 * LANES), BF16),
             vmem((N_X, *share), F32),

time: 41.2 us -> 40.9 us (level)
  no operation moved by 1% of the time
where the time goes in v6:
time: 40.9 us; the launch traced here: 40.8 us
  Pallas kernels  39.1 us (96%)
  local copies, waits for them, and re-layouts  1.7 us (4%)
    pallas_call x1, Pallas kernels, per_device(): pl.pallas_call(kernel, out_shape=jax.ShapeDtypeStruct(positions.shape, F3...  39.1 us
    unnamed x1, local copies, waits for them, and re-layouts  1.7 us

profile of v6, /device:TPU:1, one launch (start us, length us, event | category | flops | bytes accessed | tf_op | source)
XLA Modules:
  0.0 40.8 jit_solution(6369992427532554946)
XLA Ops:
  0.0 39.1 %shard_map.100 = f32[3,16384]{1,0:T(4,128)} custom-call(f32[3,16384]{1,0:T(4,128)} %pos_in.1, f32[128,128]{1,0:T(8,128)} %bitcast.2, f32[24,128]{1,0:T(8,128)} %bitcast.3, s32[1,256]{1,0:T(1,128)} %halo_in.1, s32[1,256]{1,0:T(1,128)} %tile_in.1, s32[1,1024]{1,0:T(1,128)} %slot_in.1, f32[1,16]{1,0:T(1,128)} %feedback_in.1, f32[3,128,128]{2,1,0:T(8,128)} %mixing_in.1, ...), custom_call_target="tpu_custom_call" | custom-call | tf_op jit(solution)/shard_map/pallas_call | solution.py:471
  39.1 1.7 %copy.12 = f32[3,16384]{1,0:T(4,128)} copy(f32[3,16384]{1,0:T(4,128)} %shard_map.100) | data formatting | bytes 393216

commit v7 on v6

--- a/solution.py
+++ b/solution.py
@@ -17,12 +17,13 @@
 N_X = 4
 PLANE = N_Y * OWNED
 ROWS = N_Z * PLANE
-STEPS = N_Z // 2
+SUMS = ((0, 1), (1, 2), (3, 2), (5, 2), (7, 1))
+STEPS = len(SUMS)
+DIRECT = SUMS[0][1]
 ORDER = (4, 3, 5, 2, 6, 1, 7, 0)
 TURNS = ((7, 1), (6, 1), (4, 2), (2, 2), (0, 2))
 TURNS_OF = (4, 4, 3, 3, 2, 2, 1)
 PASSED = 3
-DIRECT = 1
 LANES = 128
 QUARTERS = BLK // LANES
 PARTS = 2
@@ -71,8 +72,8 @@
             zip(inputs, (pos, mass, centre, halo, tile, slot, feedback, mixing, drive, readout))
         )
     ]
-    for copy in copies_in:
-        copy.start()
+    for i in (5, 3, 4, 2, 0, 1, 6, 7, 8, 9):
+        copies_in[i].start()
 
     me = lax.axis_index("space")
     x = lax.axis_index("halo")
@@ -108,7 +109,7 @@
     for partner in partners:
         pl.semaphore_signal(barrier, inc=1, device_id=partner, device_id_type=MESH)
 
-    for i in range(6):
+    for i in (2, 3, 4, 5):
         copies_in[i].wait()
     owner = lax.div(slot[...], OWNED)
     half = lax.rem(lax.rem(owner, 2) - core + 2, 2)
@@ -139,6 +140,8 @@
     )
     columns[...] = by_pair.T
 
+    for i in (0, 1):
+        copies_in[i].wait()
     for t in range(TILES):
         for c in range(3):
             raw[t : t + 1, c * BLK : (c + 1) * BLK] = pos[c : c + 1, t * BLK : (t + 1) * BLK]
@@ -207,11 +210,9 @@
     def block(b, carry):
         for u in range(2):
             build(b * 32 + u * 16, u)
-        for u in range(2):
             product[u] = lax.dot_general(
                 left[u], right[u], (((1,), (1,)), ((), ())), preferred_element_type=F32
             )
-        for u in range(2):
             fold(b * 32 + u * 16, u)
         return carry
 
@@ -224,35 +225,34 @@
         both = matmul(one_hot(rows_of == pair_row.astype(jnp.int32)), profiles)
         dense[first : first + count] = (both[:, :KNOTS] + both[:, KNOTS:]).reshape(count, PLANE, KNOTS)
 
-    sum_rows(0, 2 * DIRECT)
-    sum_rows(N_Z, 2 * DIRECT)
+    sum_rows(0, DIRECT)
+    sum_rows(N_Z, DIRECT)
 
     pl.semaphore_wait(barrier, len(partners))
-    for j in range(DIRECT):
-        for d in (2, 1, 3):
-            rows = pl.ds(d * OWNED, OWNED)
-            send(dense.at[pl.ds(2 * j, 2), rows], y_in.at[j, d - 1], y_send, y_recv.at[j], at(dy=d))
-            send(
-                dense.at[pl.ds(N_Z + 2 * j, 2), rows],
-                y_other.at[j, d - 1],
-                other_send,
-                other_recv.at[j],
-                at(dy=d, other=1),
-            )
-    sum_rows(N_Z + 2 * DIRECT, N_Z - 2 * DIRECT)
+    for d in (2, 1, 3):
+        rows = pl.ds(d * OWNED, OWNED)
+        send(dense.at[pl.ds(0, DIRECT), rows], y_in.at[d - 1, pl.ds(0, DIRECT)], y_send, y_recv.at[0], at(dy=d))
+        send(
+            dense.at[pl.ds(N_Z, DIRECT), rows],
+            y_other.at[d - 1],
+            other_send,
+            other_recv,
+            at(dy=d, other=1),
+        )
+    sum_rows(N_Z + DIRECT, N_Z - DIRECT)
     halves = []
-    for j in range(STEPS):
-        rows = pl.ds(0, OWNED if j < DIRECT else PLANE)
+    for j, (first, count) in enumerate(SUMS):
+        rows = pl.ds(0, PLANE if j else OWNED)
         halves.append(
             send(
-                dense.at[pl.ds(N_Z + 2 * j, 2), rows],
-                half_in.at[pl.ds(2 * j, 2), rows],
+                dense.at[pl.ds(N_Z + first, count), rows],
+                half_in.at[pl.ds(first, count), rows],
                 half_send.at[j],
                 half_recv.at[j],
                 at(other=1),
             )
         )
-    sum_rows(2 * DIRECT, N_Z - 2 * DIRECT)
+    sum_rows(DIRECT, N_Z - DIRECT)
     for i in (6, 7, 8, 9):
         copies_in[i].wait()
     for c in range(3):
@@ -271,30 +271,30 @@
         picked[first] = one_hot(rows_of + first * float(ROWS) == columns[:, 3:4])
     tile_of[...] = one_hot(lax.broadcasted_iota(jnp.int32, (TILES, PAIRS), 0) == tile[...])
 
-    for j in range(DIRECT, STEPS):
+    for j, (first, count) in enumerate(SUMS[1:], 1):
         halves[j].wait_recv()
-        turns = pl.ds(2 * j, 2)
+        turns = pl.ds(first, count)
         sums[turns] = dense[turns] + half_in[turns]
         for d in (2, 1, 3):
             send(
                 sums.at[turns, pl.ds(d * OWNED, OWNED)],
-                y_in.at[j, d - 1],
+                y_in.at[d - 1, turns],
                 y_send,
                 y_recv.at[j],
                 at(dy=d),
             )
-    for j in range(STEPS):
-        turns = slice(2 * j, 2 * j + 2)
-        if j < DIRECT:
+    for j, (first, count) in enumerate(SUMS):
+        turns = slice(first, first + count)
+        if j == 0:
             halves[j].wait_recv()
-            wait_bytes(y_other.at[j], other_recv.at[j])
-            plane = dense[turns, :OWNED] + half_in[turns, :OWNED] + y_other[j, 0] + y_other[j, 1] + y_other[j, 2]
+            wait_bytes(y_other, other_recv)
+            plane = dense[turns, :OWNED] + half_in[turns, :OWNED] + y_other[0] + y_other[1] + y_other[2]
         else:
             plane = sums[turns, :OWNED]
-        wait_bytes(y_in.at[j], y_recv.at[j])
-        plane += y_in[j, 0] + y_in[j, 1] + y_in[j, 2]
-        z_sums[2 * j : 2 * j + 2] = plane
-        for i in (2 * j, 2 * j + 1):
+        wait_bytes(y_in.at[pl.ds(0, N_Y - 1), pl.ds(first, count)], y_recv.at[j])
+        plane += y_in[0, turns] + y_in[1, turns] + y_in[2, turns]
+        z_sums[turns] = plane
+        for i in range(first, first + count):
             if ORDER[i]:
                 send(z_sums.at[i], z_in.at[i], z_send, z_recv, at(dz=ORDER[i]))
     wait_bytes(z_in, z_recv)
@@ -491,8 +491,8 @@
             vmem((2 * N_Z, PLANE, KNOTS), F32),
             vmem((N_Z, PLANE, KNOTS), F32),
             vmem((N_Z, PLANE, KNOTS), F32),
-            vmem((STEPS, N_Y - 1, 2, OWNED, KNOTS), F32),
-            vmem((DIRECT, N_Y - 1, 2, OWNED, KNOTS), F32),
+            vmem((N_Y - 1, N_Z, OWNED, KNOTS), F32),
+            vmem((N_Y - 1, DIRECT, OWNED, KNOTS), F32),
             vmem((N_Z, OWNED, KNOTS), F32),
             vmem((N_Z - 1, OWNED, KNOTS), F32),
             vmem((3, 2 * KNOTS, 2 * KNOTS), BF16),
@@ -510,7 +510,7 @@
             dma,
             dma((STEPS,)),
             dma,
-            dma((DIRECT,)),
+            dma,
             dma,
             dma,
             dma,

time: 40.9 us -> 40.7 us (level)
  no operation moved by 1% of the time
where the time goes in v7:
time: 40.7 us; the launch traced here: 40.6 us
  Pallas kernels  38.9 us (96%)
  local copies, waits for them, and re-layouts  1.7 us (4%)
    pallas_call x1, Pallas kernels, per_device(): pl.pallas_call(kernel, out_shape=jax.ShapeDtypeStruct(positions.shape, F3...  38.9 us
    unnamed x1, local copies, waits for them, and re-layouts  1.7 us

profile of v7, /device:TPU:1, one launch (start us, length us, event | category | flops | bytes accessed | tf_op | source)
XLA Modules:
  0.0 40.6 jit_solution(5190688099247106677)
XLA Ops:
  0.0 38.9 %shard_map.100 = f32[3,16384]{1,0:T(4,128)} custom-call(f32[3,16384]{1,0:T(4,128)} %pos_in.1, f32[128,128]{1,0:T(8,128)} %bitcast.2, f32[24,128]{1,0:T(8,128)} %bitcast.3, s32[1,256]{1,0:T(1,128)} %halo_in.1, s32[1,256]{1,0:T(1,128)} %tile_in.1, s32[1,1024]{1,0:T(1,128)} %slot_in.1, f32[1,16]{1,0:T(1,128)} %feedback_in.1, f32[3,128,128]{2,1,0:T(8,128)} %mixing_in.1, ...), custom_call_target="tpu_custom_call" | custom-call | tf_op jit(solution)/shard_map/pallas_call | solution.py:471
  38.9 1.7 %copy.12 = f32[3,16384]{1,0:T(4,128)} copy(f32[3,16384]{1,0:T(4,128)} %shard_map.100) | data formatting | bytes 393216
